TPU v7x, 32 devices: a whole 2x2x4 slice. The times are simulated.
32 devices in a mesh: dp: 4 (over y, x), vocab: 8 (over z, core).
Axes of the slice: x: 2, y: 2, z: 4, core: 2. Of those that a mesh axis runs over, the one named last changes fastest.
Arguments:
- hidden: bfloat16 [768, 5120], P('dp', 'vocab'), may hold values from -128 to 128
- head: bfloat16 [7168, 5120], P('vocab', 'dp'), may hold values from -0.125 to 0.125
- targets: int32 [4, 192], P('dp'), may hold values from 0 to 7167
- segments: int32 [4, 192], P('dp'), may hold values from 0 to 15, never falling along the last dimension, each value on 1 to 32 neighbouring positions
- loss_mask: int32 [4, 192], P('dp'), may hold values 0 or 1
Outputs:
- grad_hidden: bfloat16 [768, 5120], P('dp', 'vocab')
- grad_head: bfloat16 [7168, 5120], P('vocab', 'dp')
All inputs are finite; a program needn't handle non-finite values. No bound on the sum of `loss_mask` on one device may be relied on, other than what follows from the above.
Results may differ from a plain program's by a relative error of at most 0.0055.
Values may be sent and summed in bfloat16 or wider, within the bound.
A program may use at most 64 MiB of HBM per device.

v0:
```python
import jax
import jax.numpy as jnp
from jax import lax
from jax.sharding import PartitionSpec as P

loss_scale = 256.0


def body(hidden, head, targets, segments, loss_mask):
    vocab_rows = head.shape[0]
    features = lax.all_gather(hidden, "vocab", axis=1, tiled=True)
    wide_head = lax.all_gather(head, "dp", axis=1, tiled=True)
    logits = lax.dot_general(
        features, wide_head, (((1,), (1,)), ((), ())), preferred_element_type=jnp.float32
    )
    local_max = jnp.max(logits, axis=1)
    row_max = lax.pmax(local_max, "vocab")
    row_total = lax.psum(jnp.sum(jnp.exp(logits - row_max[:, None]), axis=1), "vocab")
    log_norm = row_max + jnp.log(row_total)
    mask_f = loss_mask[0].astype(jnp.float32)
    seg_ids = segments[0]
    same = (seg_ids[:, None] == seg_ids[None, :]).astype(jnp.float32)
    counts = jnp.dot(same, mask_f)
    weight = loss_scale * mask_f / jnp.maximum(counts, 1.0)
    vocab_start = lax.axis_index("vocab") * vocab_rows
    columns = vocab_start + lax.broadcasted_iota(jnp.int32, (1, vocab_rows), 1)
    onehot = (targets[0][:, None] == columns).astype(jnp.float32)
    grad_logits = (weight[:, None] * (jnp.exp(logits - log_norm[:, None]) - onehot)).astype(
        jnp.bfloat16
    )
    partial_terms = jnp.dot(grad_logits, wide_head, preferred_element_type=jnp.float32)
    grad_hidden = lax.psum_scatter(partial_terms, "vocab", scatter_dimension=1, tiled=True).astype(
        jnp.bfloat16
    )
    group_cols = lax.all_to_all(features, "dp", split_axis=1, concat_axis=0, tiled=True)
    head_total = lax.dot_general(
        lax.all_gather(grad_logits, "dp", axis=0, tiled=True),
        group_cols,
        (((0,), (0,)), ((), ())),
        preferred_element_type=jnp.float32,
    )
    grad_head = head_total.astype(jnp.bfloat16)
    return (grad_hidden, grad_head)


def solution(mesh):
    placed = (P("dp", "vocab"), P("vocab", "dp"), P("dp", None), P("dp", None), P("dp", None))
    return jax.shard_map(
        body,
        mesh=mesh,
        in_specs=placed,
        out_specs=(P("dp", "vocab"), P("vocab", "dp")),
        check_vma=False,
    )
```

profile of v0, /device:TPU:6, one launch (start us, length us, event | category | flops | bytes accessed | tf_op | source)
XLA Modules:
  0.0 271.9 jit_solution(5781431722385896448)
XLA Ops:
  7.2 0.0 copy-start.2
  7.2 0.0 copy-start.3
  7.2 0.0 all-gather.4.cloned.1.call-start
  7.2 0.7 all-gather.4.cloned.1.call-update
  7.9 0.0 all-gather.6.cloned.1.call-start
  8.0 0.7 all-gather.6.cloned.1.call-update
  8.7 0.0 all-gather.8.cloned.1.call-start
  8.7 0.0 copy-done.2
  8.8 0.0 copy-done.3
  8.8 0.2 fusion
  9.0 0.0 copy-start.1
  9.0 29.9 %all-gather.4.cloned.1.call-done = bf16[192,5120]{1,0:T(8,128)(2,1)} async-done(((bf16[192,640]{1,0:T(8,128)(2,1)}), bf16[192,5120]{1,0:T(8,128)(2,1)}) %all-gather.4.cloned.1.call-update) | async-done | bytes 1966096 | tf_op jit(solution)/shard_map/all_gather | solution.py:11
  38.9 94.6 %all-gather.6.cloned.1.call-done = bf16[896,5120]{1,0:T(8,128)(2,1)} async-done(((bf16[896,1280]{1,0:T(8,128)(2,1)}), bf16[896,5120]{1,0:T(8,128)(2,1)}) %all-gather.6.cloned.1.call-update) | async-done | bytes 9175056 | tf_op jit(solution)/shard_map/all_gather | solution.py:12
  133.5 7.5 %fusion.6 = (f32[192]{0:T(256)S(1)}, f32[192,896]{1,0:T(8,128)S(1)}) fusion(bf16[192,5120]{1,0:T(8,128)(2,1)} %all-gather.4.cloned.1.call-done, bf16[896,5120]{1,0:T(8,128)(2,1)} %all-gather.6.cloned.1.call-done), kind=kOutput, calls=%fused_computation.13 | convolution fusion | flops 1761779456 | bytes 11830016 | tf_op jit(solution)/shard_map/dot_general | solution.py:13
  141.0 16.4 %pmax.7 = f32[192]{0:T(256)S(1)} all-reduce(f32[192]{0:T(256)S(1)} %get-tuple-element.2), channel_id=1, replica_groups=mesh['dp'=4,'vocab'=8] {'vocab'}, use_global_device_ids=true, to_apply=%region_1.0 | all-reduce | flops 192 | bytes 1536 | tf_op jit(solution)/shard_map/pmax | solution.py:17
  157.3 0.3 exponential_reduce_fusion
  157.6 13.6 %psum.7 = f32[192]{0:T(256)S(1)} all-reduce(f32[192]{0:T(256)S(1)} %exponential_reduce_fusion), channel_id=1, replica_groups=mesh['dp'=4,'vocab'=8] {'vocab'}, use_global_device_ids=true, to_apply=%region_3.0 | all-reduce | flops 192 | bytes 1536 | tf_op jit(solution)/shard_map/psum | solution.py:18
  171.2 0.0 copy-done.1
  171.2 1.0 multiply_convert_fusion
  172.2 0.0 all-gather.8.cloned.1.call-update
  172.2 0.0 reduce-scatter.2.cloned.1.call-start
  172.3 7.9 %fusion.7 = f32[192,5120]{1,0:T(8,128)} fusion(bf16[192,896]{1,0:T(8,128)(2,1)} %multiply_convert_fusion, bf16[896,5120]{1,0:T(8,128)(2,1)} %all-gather.6.cloned.1.call-done), kind=kOutput, calls=%fused_computation.14 | convolution fusion | flops 1761607680 | bytes 13451264 | tf_op jit(solution)/shard_map/dot_general | solution.py:31
  180.1 0.0 copy-start
  180.1 0.0 reduce-scatter.2.cloned.1.call-update
  180.2 1.5 copy-done
  181.7 0.1 copy.11
  181.8 33.4 %all_to_all.19 = bf16[192,4,1280]{2,0,1:T(8,128)(2,1)S(1)} all-to-all(bf16[192,4,1280]{2,0,1:T(8,128)(2,1)S(1)} %bitcast.20), channel_id=1, replica_groups=mesh['dp'=4,'vocab'=8] {'dp'}, dimensions={1} | all-to-all | bytes 3932160 | tf_op jit(solution)/shard_map/all_to_all | solution.py:35
  215.2 0.6 all-gather.8.cloned.1.call-done
  215.7 4.7 %convolution_convert_fusion = bf16[896,1280]{1,0:T(8,128)(2,1)} fusion(bf16[768,896]{1,0:T(8,128)(2,1)} %all-gather.8.cloned.1.call-done, bf16[768,1280]{1,0:T(8,128)(2,1)S(1)} %bitcast.22), kind=kOutput, calls=%fused_computation | convolution fusion | flops 1762754560 | bytes 5636096 | tf_op jit(solution)/shard_map/dot_general | solution.py:36
  220.4 43.2 %reduce-scatter.2.cloned.1.call-done = f32[192,640]{1,0:T(8,128)} async-done(((f32[192,5120]{1,0:T(8,128)}), f32[192,640]{1,0:T(8,128)}) %reduce-scatter.2.cloned.1.call-update) | async-done | bytes 491536 | tf_op jit(solution)/shard_map/reduce_scatter | solution.py:32
  263.6 1.8 convert_element_type.23
  (4 shorter events, 0.0 us)
Async XLA Ops:
  7.2 1.6 copy-start.2
  7.2 1.6 copy-start.3
  7.2 31.7 %all-gather.4.cloned.1.call-start = ((), (), s32[]{:S(2)}) async-start(), calls=%async_computation.2 | async-start | bytes 2211840 | tf_op jit(solution)/shard_map/all_gather | solution.py:11
  7.9 125.6 %all-gather.6.cloned.1.call-start = ((), (), s32[]{:S(2)}) async-start(), calls=%async_computation.3 | async-start | bytes 11468800 | tf_op jit(solution)/shard_map/all_gather | solution.py:12
  8.7 207.1 %all-gather.8.cloned.1.call-start = ((), (), s32[]{:S(2)}) async-start(), calls=%async_computation.5 | async-start | bytes 1720320 | tf_op jit(solution)/shard_map/all_gather | solution.py:37
  9.0 162.2 %copy-start.1 = (s32[1,192]{1,0:T(1,128)S(1)}, s32[1,192]{1,0:T(1,128)}, u32[]{:S(2)}) copy-start(s32[1,192]{1,0:T(1,128)} %param.7) | copy-start | bytes 2308
  172.2 91.4 %reduce-scatter.2.cloned.1.call-start = ((), (), s32[]{:S(2)}) async-start(), calls=%async_computation.4 | async-start | bytes 4423680 | tf_op jit(solution)/shard_map/reduce_scatter | solution.py:32
  180.1 1.5 copy-start
Sparse Core Ops, SparseCore 0:
  9.6 29.2 all-gather.3
  40.7 92.7 all-gather.5
  172.3 43.3 all-gather.7
  217.9 45.6 reduce-scatter.1
where the time goes:
time: 274 us; the launch traced here: 272 us
  waiting for transfers between devices  170 us (62%)
  blocking collectives  63.3 us (23%)
  matrix products  20.3 us (7%)
  between operations  13.8 us (5%)
  other arithmetic  3.02 us (1%)
    all_gather x1, waiting for transfers between devices, body(): wide_head = lax.all_gather(head, 'dp', axis=1, tiled=True)  94.6 us
    reduce_scatter x1, waiting for transfers between devices, body(): lax.psum_scatter(partial_terms, 'vocab', scatter_dimension=1, tiled=True)  43.2 us
    all_to_all x1, blocking collectives, body(): lax.all_to_all(features, 'dp', split_axis=1, concat_axis=0, tiled=True)  33.4 us
    all_gather x1, waiting for transfers between devices, body(): features = lax.all_gather(hidden, 'vocab', axis=1, tiled=True)  29.9 us
    pmax x1, blocking collectives, body(): row_max = lax.pmax(local_max, 'vocab')  16.4 us
    psum x1, blocking collectives, body(): lax.psum(jnp.sum(jnp.exp(logits - row_max[:, None]), axis=1), 'vocab')  13.6 us
    dot_general x1, matrix products, body(): jnp.dot(grad_logits, wide_head, preferred_element_type=jnp.float32)  7.87 us
    dot_general x1, matrix products, body(): lax.dot_general(features, wide_head, (((1,), (1,)), ((), ())), preferred_...  7.48 us
  transfers between devices with their start and end apart: 4, of which 4 were waited for; matrix products, arithmetic and copies ran while one was open for 5% of the time, Pallas kernels for 0%

commit v1 on v0

--- a/solution.py
+++ b/solution.py
@@ -1,9 +1,425 @@
+import functools
+
 import jax
 import jax.numpy as jnp
 from jax import lax
+from jax.experimental import pallas as pl
+from jax.experimental.pallas import tpu as pltpu
 from jax.sharding import PartitionSpec as P
 
 loss_scale = 256.0
+MESH = pl.DeviceIdType.MESH
+CHUNKS = 2
+
+
+def token_weight(segments, loss_mask):
+    mask_f = loss_mask[0].astype(jnp.float32)
+    seg_ids = segments[0]
+    same = (seg_ids[:, None] == seg_ids[None, :]).astype(jnp.float32)
+    counts = jnp.sum(same * mask_f[None, :], axis=1)
+    return loss_scale * mask_f / jnp.maximum(counts, 1.0)
+
+
+def kernel(
+    rows, width, vocab_rows,
+    hidden_ref, head_hbm, target_ref, weight_ref,
+    out_hidden, out_head,
+    head, feats, mine, part, recv_a, recv_b, tile, stats, grads,
+    q_keep, q_pair, q_pair_in, q_plane, q_plane_in, q_line, ghead,
+    head_sem, out_sem, own_sem,
+    line_s, line_r, plane_s, plane_r, pair_s, pair_r,
+    red_s, red_r, stat_s, stat_r, gat_s, gat_r,
+    qpair_s, qpair_r, qplane_s, qplane_r, qline_s, qline_r,
+):
+    g = lax.axis_index("dp")
+    v = lax.axis_index("vocab")
+    z, c = v // 2, v % 2
+    gy, gx = g // 2, g % 2
+    xn, yn, dn = gy * 2 + 1 - gx, (1 - gy) * 2 + gx, (1 - gy) * 2 + 1 - gx
+    sib = z * 2 + 1 - c
+    half = rows // 2
+    col = pl.multiple_of(c * width, 128)
+    other_col = pl.multiple_of((1 - c) * width, 128)
+    sends = []
+
+    def remote(src, dst, ssem, rsem, dev):
+        return pltpu.make_async_remote_copy(
+            src_ref=src, dst_ref=dst, send_sem=ssem, recv_sem=rsem,
+            device_id=dev, device_id_type=MESH,
+        )
+
+    def bin_rows(b, off=0, n=None):
+        n = rows if n is None else n
+        return pl.ds(pl.multiple_of(b * rows + off, 16), n)
+
+    head_copy = pltpu.make_async_copy(head_hbm, head, head_sem)
+    head_copy.start()
+
+    barrier = pltpu.get_barrier_semaphore()
+    for p in (xn, yn, dn):
+        pl.semaphore_signal(barrier, inc=1, device_id=(p, v), device_id_type=MESH)
+    for i in range(1, 8):
+        pl.semaphore_signal(barrier, inc=1, device_id=(g, lax.rem(v + i, 8)), device_id_type=MESH)
+    for k in range(CHUNKS):
+        feats[k, z] = hidden_ref[k * rows:(k + 1) * rows, :]
+    tile[...] = jnp.ones_like(tile)
+    pl.semaphore_wait(barrier, 10)
+
+    def line_copy(k, right, d):
+        step = 1 if right else -1
+        s = z - step * d
+        return remote(
+            feats.at[k, s], feats.at[k, s], line_s.at[k, int(right), d], line_r.at[k, int(right), d],
+            (g, (z + step) * 2 + c),
+        )
+
+    def line_ok(right, d):
+        if right:
+            return (z >= d) & (z < 3)
+        return (z + d <= 3) & (z > 0)
+
+    def line_send(k, right, d):
+        @pl.when(line_ok(right, d))
+        def _():
+            line_copy(k, right, d).start()
+
+    def line_send_wait(k, right, d):
+        @pl.when(line_ok(right, d))
+        def _():
+            line_copy(k, right, d).wait_send()
+
+    def plane_copy(k, s):
+        return remote(
+            feats.at[k, s], mine.at[k, bin_rows(g), pl.ds(col, width)],
+            plane_s.at[k, s], plane_r.at[k, g], (s, v),
+        )
+
+    def own_copy(k):
+        return pltpu.make_async_copy(
+            feats.at[k, g], mine.at[k, bin_rows(g), pl.ds(col, width)], own_sem.at[k]
+        )
+
+    def plane_send(k, s):
+        @pl.when(s == g)
+        def _():
+            own_copy(k).start()
+
+        @pl.when(s != g)
+        def _():
+            plane_copy(k, s).start()
+
+    def line_recv(k, right, d):
+        step = 1 if right else -1
+        s = z - step * d
+        here = (z >= d) if right else (z + d <= 3)
+
+        @pl.when(here)
+        def _():
+            remote(
+                feats.at[k, s], feats.at[k, s], line_s.at[k, int(right), d - 1],
+                line_r.at[k, int(right), d - 1], (g, v),
+            ).wait_recv()
+            if d < 3:
+                line_send(k, right, d)
+            plane_send(k, s)
+
+    def pair_copy(k, b):
+        at = mine.at[k, bin_rows(b), pl.ds(col, width)]
+        return remote(at, at, pair_s.at[k, b], pair_r.at[k, b], (g, sib))
+
+    def hidden_line(k):
+        for d in (1, 2, 3):
+            line_recv(k, True, d)
+            line_recv(k, False, d)
+
+    def hidden_plane(k):
+        own_copy(k).wait()
+        pair_copy(k, g).start()
+        for p in (xn, yn, dn):
+            at = mine.at[k, bin_rows(p), pl.ds(col, width)]
+            remote(at, at, plane_s.at[k, p], plane_r.at[k, p], (p, v)).wait_recv()
+            pair_copy(k, p).start()
+        for p in (g, xn, yn, dn):
+            at = mine.at[k, bin_rows(p), pl.ds(other_col, width)]
+            remote(at, at, pair_s.at[k, p], pair_r.at[k, p], (g, sib)).wait_recv()
+
+    def hidden_finish(k):
+        for right in (True, False):
+            for d in (0, 1, 2):
+                line_send_wait(k, right, d)
+        for s in range(4):
+            @pl.when(s != g)
+            def _():
+                plane_copy(k, s).wait_send()
+        for p in (g, xn, yn, dn):
+            pair_copy(k, p).wait_send()
+
+    def red_copy(k, way, i):
+        buf = (recv_a, recv_b)[way]
+        off = way * half
+        first, second = ((xn, yn), (yn, xn))[way]
+        b = (dn, first, second)[i]
+        dev = (first, first, second)[i]
+        return remote(
+            part.at[k, bin_rows(b, off, half)], buf.at[k, i],
+            red_s.at[k, way, i], red_r.at[k, way, i], (dev, v),
+        )
+
+    def logits_start(k):
+        part[k] = lax.dot_general(
+            mine[k], head[...], (((1,), (1,)), ((), ())), preferred_element_type=jnp.float32
+        )
+        for i in (0, 1):
+            for way in (0, 1):
+                red_copy(k, way, i).start()
+
+    def logits_forward(k):
+        for way in (0, 1):
+            buf = (recv_a, recv_b)[way]
+            second = (yn, xn)[way]
+            red_copy(k, way, 0).wait_recv()
+            at = bin_rows(second, way * half, half)
+            part[k, at] = part[k, at] + buf[k, 0]
+            red_copy(k, way, 2).start()
+
+    def stat_copy(k, i):
+        peer = lax.rem(v + i, 8)
+        return remote(stats.at[k, v], stats.at[k, v], stat_s.at[k, i - 1], stat_r.at[k, i - 1], (g, peer))
+
+    def logits_finish(k):
+        for i in (1, 2):
+            for way in (0, 1):
+                red_copy(k, way, i).wait_recv()
+        for way in (0, 1):
+            buf = (recv_a, recv_b)[way]
+            at = bin_rows(g, way * half, half)
+            part[k, at] = part[k, at] + buf[k, 1] + buf[k, 2]
+        logits = part[k, bin_rows(g)]
+        top = jnp.max(logits, axis=1, keepdims=True)
+        total = jnp.sum(jnp.exp(logits - top), axis=1, keepdims=True)
+        lane = lax.broadcasted_iota(jnp.int32, (rows, 128), 1)
+        tile[0:rows, :] = jnp.where(lane == 0, top, total)
+        stats[k, v] = tile[...].T[0:8, :]
+        for i in range(1, 8):
+            stat_copy(k, i).start()
+
+    def gat_copy(k, to_y, i):
+        dev = yn if to_y else xn
+        if i == 2:
+            b, off = (xn, 0) if to_y else (yn, half)
+        else:
+            b, off = g, ((half, 0) if to_y else (0, half))[i]
+        at = grads.at[k, bin_rows(b, off, half)]
+        return remote(at, at, gat_s.at[k, int(to_y), i], gat_r.at[k, int(to_y), i], (dev, v))
+
+    def gat_wait(k, to_y, i):
+        gat_copy(k, to_y, i).wait_recv()
+
+    def grads_start(k):
+        for i in range(1, 8):
+            stat_copy(k, i).wait_recv()
+        tops = stats[k, :, 0, :]
+        totals = stats[k, :, 1, :]
+        top = jnp.max(tops, axis=0, keepdims=True)
+        total = jnp.sum(totals * jnp.exp(tops - top), axis=0, keepdims=True)
+        norm = jnp.broadcast_to(top + jnp.log(total), (128, 128)).T[0:rows, 0:1]
+        logits = part[k, bin_rows(g)]
+        weight = weight_ref[k * rows:(k + 1) * rows, :]
+        target = target_ref[k * rows:(k + 1) * rows, :] - v * vocab_rows
+        columns = lax.broadcasted_iota(jnp.int32, (rows, vocab_rows), 1)
+        onehot = (target == columns).astype(jnp.float32)
+        grads[k, bin_rows(g)] = (weight * (jnp.exp(logits - norm) - onehot)).astype(jnp.bfloat16)
+        for i in (0, 1):
+            for to_y in (False, True):
+                gat_copy(k, to_y, i).start()
+
+    def grads_forward(k):
+        gat_wait(k, False, 0)
+        gat_copy(k, True, 2).start()
+        gat_wait(k, True, 0)
+        gat_copy(k, False, 2).start()
+
+    def qpair_copy(k, b):
+        return remote(q_pair.at[k, b], q_pair_in.at[k, b], qpair_s.at[k, b], qpair_r.at[k, b], (g, sib))
+
+    def qplane_copy(k, b):
+        return remote(q_plane.at[k, b], q_plane_in.at[k, g], qplane_s.at[k, b], qplane_r.at[k, g], (b, v))
+
+    def qline_copy(k, s):
+        return remote(
+            q_plane_in.at[k, s], q_line.at[k, z], qline_s.at[k, s], qline_r.at[k, z], (g, s * 2 + c)
+        )
+
+    def terms_start(k, b):
+        grad = grads[k, bin_rows(b)]
+        q_pair[k, b] = jnp.dot(
+            grad, head[:, pl.ds(other_col, width)], preferred_element_type=jnp.float32
+        ).astype(jnp.bfloat16)
+        qpair_copy(k, b).start()
+        q_keep[k, b] = jnp.dot(grad, head[:, pl.ds(col, width)], preferred_element_type=jnp.float32)
+
+    def line_start(k, s):
+        @pl.when(s == z)
+        def _():
+            q_line[k, z] = q_plane_in[k, s]
+
+        @pl.when(s != z)
+        def _():
+            qline_copy(k, s).start()
+
+    def terms_send(k, b, own):
+        qpair_copy(k, b).wait_recv()
+        total = (q_keep[k, b] + q_pair_in[k, b].astype(jnp.float32)).astype(jnp.bfloat16)
+        if own:
+            q_plane_in[k, b] = total
+            line_start(k, b)
+        else:
+            q_plane[k, b] = total
+            qplane_copy(k, b).start()
+
+    def terms_line(k):
+        for p in (xn, yn, dn):
+            remote(q_plane.at[k, p], q_plane_in.at[k, p], qplane_s.at[k, p], qplane_r.at[k, p], (p, v)).wait_recv()
+            line_start(k, p)
+
+    def terms_finish(k):
+        for s in range(4):
+            @pl.when(s != z)
+            def _():
+                remote(q_line.at[k, s], q_line.at[k, s], qline_s.at[k, s], qline_r.at[k, s], (g, v)).wait_recv()
+        total = q_line[k, 0].astype(jnp.float32)
+        for s in range(1, 4):
+            total = total + q_line[k, s].astype(jnp.float32)
+        out_hidden[k * rows:(k + 1) * rows, :] = total.astype(jnp.bfloat16)
+
+    def terms_round(k):
+        terms_start(k, g)
+        gat_wait(k, False, 1)
+        terms_start(k, xn)
+        terms_send(k, g, True)
+        gat_wait(k, True, 1)
+        terms_start(k, yn)
+        terms_send(k, xn, False)
+        gat_wait(k, False, 2)
+        gat_wait(k, True, 2)
+        terms_start(k, dn)
+        terms_send(k, yn, False)
+        terms_send(k, dn, False)
+
+    for k in range(CHUNKS):
+        line_send(k, True, 0)
+        line_send(k, False, 0)
+        plane_send(k, z)
+    hidden_line(0)
+    hidden_plane(0)
+    head_copy.wait()
+    logits_start(0)
+    hidden_line(1)
+    hidden_plane(1)
+    logits_start(1)
+    logits_forward(0)
+    logits_forward(1)
+    logits_finish(0)
+    grads_start(0)
+    logits_finish(1)
+    grads_forward(0)
+    grads_start(1)
+    terms_round(0)
+    grads_forward(1)
+    terms_line(0)
+    terms_round(1)
+    terms_line(1)
+
+    tiles = 4
+    tile_cols = ghead.shape[1] // tiles
+    outs = []
+    for n in range(tiles):
+        at = pl.ds(n * tile_cols, tile_cols)
+        total = None
+        for k in range(CHUNKS):
+            term = lax.dot_general(
+                grads[k], mine[k, :, at], (((0,), (0,)), ((), ())), preferred_element_type=jnp.float32
+            )
+            total = term if total is None else total + term
+        ghead[:, at] = total.astype(jnp.bfloat16)
+    out_copy = pltpu.make_async_copy(ghead, out_head, out_sem)
+    out_copy.start()
+
+    for k in range(CHUNKS):
+        terms_finish(k)
+    for k in range(CHUNKS):
+        hidden_finish(k)
+        for way in (0, 1):
+            for i in (0, 1, 2):
+                red_copy(k, way, i).wait_send()
+                gat_copy(k, way, i).wait_send()
+        for i in range(1, 8):
+            stat_copy(k, i).wait_send()
+        for p in (g, xn, yn, dn):
+            qpair_copy(k, p).wait_send()
+        for p in (xn, yn, dn):
+            qplane_copy(k, p).wait_send()
+        for s in range(4):
+            @pl.when(s != z)
+            def _():
+                qline_copy(k, s).wait_send()
+    out_copy.wait()
+
+
+def fused(hidden, head, targets, segments, loss_mask):
+    tokens, width = hidden.shape
+    vocab_rows, head_width = head.shape
+    rows = tokens // CHUNKS
+    half = rows // 2
+    weight = token_weight(segments, loss_mask)[:, None]
+    target = targets[0][:, None]
+    bf16, f32 = jnp.bfloat16, jnp.float32
+    dma = pltpu.SemaphoreType.DMA
+    vmem = pl.BlockSpec(memory_space=pltpu.VMEM)
+    hbm = pl.BlockSpec(memory_space=pl.ANY)
+    K = CHUNKS
+    return pl.pallas_call(
+        functools.partial(kernel, rows, width, vocab_rows),
+        out_shape=(
+            jax.ShapeDtypeStruct(hidden.shape, bf16),
+            jax.ShapeDtypeStruct(head.shape, bf16),
+        ),
+        in_specs=[vmem, hbm, vmem, vmem],
+        out_specs=(vmem, hbm),
+        scratch_shapes=[
+            pltpu.VMEM(head.shape, bf16),
+            pltpu.VMEM((K, 4, rows, width), bf16),
+            pltpu.VMEM((K, 4 * rows, head_width), bf16),
+            pltpu.VMEM((K, 4 * rows, vocab_rows), f32),
+            pltpu.VMEM((K, 3, half, vocab_rows), f32),
+            pltpu.VMEM((K, 3, half, vocab_rows), f32),
+            pltpu.VMEM((128, 128), f32),
+            pltpu.VMEM((K, 8, 8, 128), f32),
+            pltpu.VMEM((K, 4 * rows, vocab_rows), bf16),
+            pltpu.VMEM((K, 4, rows, width), f32),
+            pltpu.VMEM((K, 4, rows, width), bf16),
+            pltpu.VMEM((K, 4, rows, width), bf16),
+            pltpu.VMEM((K, 4, rows, width), bf16),
+            pltpu.VMEM((K, 4, rows, width), bf16),
+            pltpu.VMEM((K, 4, rows, width), bf16),
+            pltpu.VMEM(head.shape, bf16),
+            dma, dma, dma((K,)),
+            dma((K, 2, 3)), dma((K, 2, 3)),
+            dma((K, 4)), dma((K, 4)), dma((K, 4)), dma((K, 4)),
+            dma((K, 2, 3)), dma((K, 2, 3)),
+            dma((K, 7)), dma((K, 7)),
+            dma((K, 2, 3)), dma((K, 2, 3)),
+            dma((K, 4)), dma((K, 4)), dma((K, 4)), dma((K, 4)), dma((K, 4)), dma((K, 4)),
+        ],
+        compiler_params=pltpu.CompilerParams(
+            collective_id=0, has_side_effects=True, vmem_limit_bytes=56 * 1024 * 1024
+        ),
+        cost_estimate=pl.CostEstimate(
+            flops=3 * 2 * 4 * tokens * vocab_rows * head_width,
+            bytes_accessed=4 * vocab_rows * head_width,
+            transcendentals=2 * tokens * vocab_rows,
+        ),
+    )(hidden, head, target, weight)
 
 
 def body(hidden, head, targets, segments, loss_mask):
@@ -17,11 +433,7 @@
     row_max = lax.pmax(local_max, "vocab")
     row_total = lax.psum(jnp.sum(jnp.exp(logits - row_max[:, None]), axis=1), "vocab")
     log_norm = row_max + jnp.log(row_total)
-    mask_f = loss_mask[0].astype(jnp.float32)
-    seg_ids = segments[0]
-    same = (seg_ids[:, None] == seg_ids[None, :]).astype(jnp.float32)
-    counts = jnp.dot(same, mask_f)
-    weight = loss_scale * mask_f / jnp.maximum(counts, 1.0)
+    weight = token_weight(segments, loss_mask)
     vocab_start = lax.axis_index("vocab") * vocab_rows
     columns = vocab_start + lax.broadcasted_iota(jnp.int32, (1, vocab_rows), 1)
     onehot = (targets[0][:, None] == columns).astype(jnp.float32)
@@ -39,14 +451,14 @@
         (((0,), (0,)), ((), ())),
         preferred_element_type=jnp.float32,
     )
-    grad_head = head_total.astype(jnp.bfloat16)
-    return (grad_hidden, grad_head)
+    return (grad_hidden, head_total.astype(jnp.bfloat16))
 
 
 def solution(mesh):
     placed = (P("dp", "vocab"), P("vocab", "dp"), P("dp", None), P("dp", None), P("dp", None))
+    fits = mesh.shape["dp"] == 4 and mesh.shape["vocab"] == 8
     return jax.shard_map(
-        body,
+        fused if fits else body,
         mesh=mesh,
         in_specs=placed,
         out_specs=(P("dp", "vocab"), P("vocab", "dp")),

time: 274 us -> 110 us (0.40)
  waiting for transfers between devices: 170 us -> 0 us
  Pallas kernels: 0 us -> 99.9 us
  blocking collectives: 63.3 us -> 0 us
  matrix products: 20.3 us -> 0 us
  between operations: 13.8 us -> 0.65 us
  local copies, waits for them, and re-layouts: 1.66 us -> 7.05 us
    all_gather x3 -> x0, waiting for transfers between devices: 125 us -> none  [the longest x1 94.6 us: body(): wide_head = lax.all_gather(head, 'dp', axis=1, tiled=True)]
    pallas_call x0 -> x1, Pallas kernels: none -> 99.9 us  [fused(): pl.pallas_call(functools.partial(kernel, rows, width, vocab_rows), out_sh...]
    reduce_scatter x1 -> x0, waiting for transfers between devices: 43.2 us -> none  [body(): lax.psum_scatter(partial_terms, 'vocab', scatter_dimension=1, tiled=True)]
    all_to_all x1 -> x0, blocking collectives: 33.4 us -> none  [body(): lax.all_to_all(features, 'dp', split_axis=1, concat_axis=0, tiled=True)]
    dot_general x4 -> x0, matrix products: 20.3 us -> none  [the longest x1 7.87 us: body(): jnp.dot(grad_logits, wide_head, preferred_element_type=jnp.float32)]
    pmax x1 -> x0, blocking collectives: 16.4 us -> none  [body(): row_max = lax.pmax(local_max, 'vocab')]
    psum x1 -> x0, blocking collectives: 13.6 us -> none  [body(): lax.psum(jnp.sum(jnp.exp(logits - row_max[:, None]), axis=1), 'vocab')]
    unnamed x8 -> x2, local copies, waits for them, and re-layouts: 1.53 us -> 4.84 us
  transfers between devices with their start and end apart: 4 -> 0, of which waited for: 4 -> 0; matrix products, arithmetic and copies ran while one was open for 5% -> 0% of each run, Pallas kernels for 0% -> 0%
where the time goes in v1:
time: 110 us
  Pallas kernels  99.9 us (91%)
  local copies, waits for them, and re-layouts  7.05 us (6%)
  other arithmetic  2.31 us (2%)
    pallas_call x1, Pallas kernels, fused(): pl.pallas_call(functools.partial(kernel, rows, width, vocab_rows), out_sh...  99.9 us
    unnamed x2, local copies, waits for them, and re-layouts  4.84 us

profile of v1, /device:TPU:6, one launch (start us, length us, event | category | flops | bytes accessed | tf_op | source)
XLA Modules:
  0.0 109.9 jit_solution(2717188982891077615)
XLA Ops:
  0.6 0.7 convert_element_type.13
  1.3 0.9 select_reduce_fusion
  2.3 0.7 bitcast_divide_fusion
  3.0 0.8 copy.14.weight_ref
  3.7 1.4 %copy.13.target_ref = s32[192,1]{1,0:T(8,128)} copy(s32[192,1]{0,1:T(1,128)} %bitcast.9) | data formatting | bytes 1536 | tf_op jit(solution)/shard_map/broadcast_in_dim;squeeze | solution.py:375
  5.2 99.9 %shard_map.68 = (bf16[192,640]{1,0:T(8,128)(2,1)}, bf16[896,1280]{1,0:T(8,128)(2,1)}) custom-call(bf16[192,640]{1,0:T(8,128)(2,1)} %hidden_ref.1, bf16[896,1280]{1,0:T(8,128)(2,1)} %head_hbm.1, s32[192,1]{1,0:T(8,128)} %copy.13.target_ref, f32[192,1]{1,0:T(8,128)} %copy.14.weight_ref), custom_call_target="tpu_custom_call" | custom-call | flops 5284823040 | bytes 4587520 | tf_op jit(solution)/shard_map/pallas_call | solution.py:381
  105.0 1.7 %copy.17 = bf16[192,640]{1,0:T(8,128)(2,1)} copy(bf16[192,640]{1,0:T(8,128)(2,1)} %get-tuple-element.4) | data formatting | bytes 491520
  106.7 3.2 %copy.18 = bf16[896,1280]{1,0:T(8,128)(2,1)} copy(bf16[896,1280]{1,0:T(8,128)(2,1)} %get-tuple-element.5) | data formatting | bytes 4587520
  (1 shorter events, 0.0 us)

commit v2 on v1

v2 whole, which is shorter than its diff:
```python
import functools

import jax
import jax.numpy as jnp
from jax import lax
from jax.experimental import pallas as pl
from jax.experimental.pallas import tpu as pltpu
from jax.sharding import PartitionSpec as P

loss_scale = 256.0
MESH = pl.DeviceIdType.MESH
CHUNKS = 3


def token_weight(segments, loss_mask):
    mask_f = loss_mask[0].astype(jnp.float32)
    seg_ids = segments[0]
    same = (seg_ids[:, None] == seg_ids[None, :]).astype(jnp.float32)
    counts = jnp.sum(same * mask_f[None, :], axis=1)
    return loss_scale * mask_f / jnp.maximum(counts, 1.0)


def kernel(
    rows, width, vocab_rows,
    hidden_hbm, head_hbm, target_ref, segment_ref, mask_ref,
    out_hidden, out_head,
    head, feats, mine, part, recv_a, recv_b, tile, stats, grads, weights, target_col,
    q_keep, q_pair, q_pair_in, q_plane, q_plane_in, q_line, ghead,
    head_sem, out_sem, hidden_sem, own_sem,
    line_s, line_r, plane_s, plane_r, pair_s, pair_r,
    red_s, red_r, stat_s, stat_r, gat_s, gat_r,
    qpair_s, qpair_r, qplane_s, qplane_r, qline_s, qline_r,
):
    g = lax.axis_index("dp")
    v = lax.axis_index("vocab")
    z, c = v // 2, v % 2
    gy, gx = g // 2, g % 2
    xn, yn, dn = gy * 2 + 1 - gx, (1 - gy) * 2 + gx, (1 - gy) * 2 + 1 - gx
    peers = (g, xn, yn, dn)
    sib = z * 2 + 1 - c
    half = rows // 2
    col = pl.multiple_of(c * width, 128)
    other_col = pl.multiple_of((1 - c) * width, 128)
    f32, bf16 = jnp.float32, jnp.bfloat16

    def remote(src, dst, ssem, rsem, dev):
        return pltpu.make_async_remote_copy(
            src_ref=src, dst_ref=dst, send_sem=ssem, recv_sem=rsem,
            device_id=dev, device_id_type=MESH,
        )

    def place(r, off=0, n=None):
        return pl.ds(r * rows + off, rows if n is None else n)

    def hidden_copy(k):
        return pltpu.make_async_copy(
            hidden_hbm.at[pl.ds(k * rows, rows)], feats.at[k, z], hidden_sem.at[k]
        )

    for k in range(CHUNKS):
        hidden_copy(k).start()
    head_copy = pltpu.make_async_copy(head_hbm, head, head_sem)
    head_copy.start()

    barrier = pltpu.get_barrier_semaphore()
    for p in (xn, yn, dn):
        pl.semaphore_signal(barrier, inc=1, device_id=(p, v), device_id_type=MESH)
    for i in range(1, 8):
        pl.semaphore_signal(barrier, inc=1, device_id=(g, lax.rem(v + i, 8)), device_id_type=MESH)
    tile[...] = jnp.ones_like(tile)
    for k in range(CHUNKS):
        hidden_copy(k).wait()
    pl.semaphore_wait(barrier, 10)

    def line_copy(k, right, d):
        step = 1 if right else -1
        s = z - step * d
        return remote(
            feats.at[k, s], feats.at[k, s], line_s.at[k, int(right), d], line_r.at[k, int(right), d],
            (g, (z + step) * 2 + c),
        )

    def line_ok(right, d):
        if right:
            return (z >= d) & (z < 3)
        return (z + d <= 3) & (z > 0)

    def line_send(k, right, d):
        @pl.when(line_ok(right, d))
        def _():
            line_copy(k, right, d).start()

    def line_send_wait(k, right, d):
        @pl.when(line_ok(right, d))
        def _():
            line_copy(k, right, d).wait_send()

    def plane_copy(k, s):
        r = (gx + s) % 2 + 2 * ((gy + s // 2) % 2)
        at = pl.ds(pl.multiple_of(r * rows, 16), rows)
        return remote(
            feats.at[k, s], mine.at[k, at, pl.ds(col, width)], plane_s.at[k, s], plane_r.at[k, r], (s, v)
        )

    def own_copy(k):
        return pltpu.make_async_copy(feats.at[k, g], mine.at[k, place(0), pl.ds(col, width)], own_sem.at[k])

    def plane_send(k, s):
        @pl.when(s == g)
        def _():
            own_copy(k).start()

        @pl.when(s != g)
        def _():
            plane_copy(k, s).start()

    def line_recv(k, right, d):
        step = 1 if right else -1
        s = z - step * d
        here = (z >= d) if right else (z + d <= 3)

        @pl.when(here)
        def _():
            remote(
                feats.at[k, s], feats.at[k, s], line_s.at[k, int(right), d - 1],
                line_r.at[k, int(right), d - 1], (g, v),
            ).wait_recv()
            if d < 3:
                line_send(k, right, d)
            plane_send(k, s)

    def pair_copy(k, r):
        at = mine.at[k, place(r), pl.ds(col, width)]
        return remote(at, at, pair_s.at[k, r], pair_r.at[k, r], (g, sib))

    def hidden_first(k):
        line_send(k, True, 0)
        line_send(k, False, 0)
        plane_send(k, z)

    def hidden_line(k):
        for d in (1, 2, 3):
            line_recv(k, True, d)
            line_recv(k, False, d)

    def hidden_plane(k):
        own_copy(k).wait()
        pair_copy(k, 0).start()
        for r in (1, 2, 3):
            at = mine.at[k, place(r), pl.ds(col, width)]
            remote(at, at, plane_s.at[k, r], plane_r.at[k, r], (peers[r], v)).wait_recv()
            pair_copy(k, r).start()
        for r in range(4):
            at = mine.at[k, place(r), pl.ds(other_col, width)]
            remote(at, at, pair_s.at[k, r], pair_r.at[k, r], (g, sib)).wait_recv()

    def hidden_finish(k):
        for right in (True, False):
            for d in (0, 1, 2):
                line_send_wait(k, right, d)
        for s in range(4):
            @pl.when(s != g)
            def _():
                plane_copy(k, s).wait_send()
        for r in range(4):
            pair_copy(k, r).wait_send()

    def red_copy(k, way, i):
        buf = (recv_a, recv_b)[way]
        first, second = ((1, 2), (2, 1))[way]
        r = (3, first, second)[i]
        dev = peers[(first, first, second)[i]]
        return remote(
            part.at[k, place(r, way * half, half)], buf.at[k, i],
            red_s.at[k, way, i], red_r.at[k, way, i], (dev, v),
        )

    def logits_start(k):
        part[k] = lax.dot_general(
            mine[k], head[...], (((1,), (1,)), ((), ())), preferred_element_type=f32
        )
        for i in (0, 1):
            for way in (0, 1):
                red_copy(k, way, i).start()

    def logits_forward(k):
        for way in (0, 1):
            buf = (recv_a, recv_b)[way]
            red_copy(k, way, 0).wait_recv()
            at = place((2, 1)[way], way * half, half)
            part[k, at] = part[k, at] + buf[k, 0]
            red_copy(k, way, 2).start()

    def stat_copy(k, i):
        peer = lax.rem(v + i, 8)
        return remote(stats.at[k, v], stats.at[k, v], stat_s.at[k, i - 1], stat_r.at[k, i - 1], (g, peer))

    def logits_finish(k):
        for i in (1, 2):
            for way in (0, 1):
                red_copy(k, way, i).wait_recv()
        for way in (0, 1):
            buf = (recv_a, recv_b)[way]
            at = place(0, way * half, half)
            part[k, at] = part[k, at] + buf[k, 1] + buf[k, 2]
        logits = part[k, place(0)]
        top = jnp.max(logits, axis=1, keepdims=True)
        total = jnp.sum(jnp.exp(logits - top), axis=1, keepdims=True)
        lane = lax.broadcasted_iota(jnp.int32, (rows, 128), 1)
        tile[0:rows, :] = jnp.where(lane == 0, top, total)
        stats[k, v] = tile[...].T[0:8, :]
        for i in range(1, 8):
            stat_copy(k, i).start()

    def gat_copy(k, to_y, i):
        dev = yn if to_y else xn
        if i == 2:
            src, dst, off = (1, 3, 0) if to_y else (2, 3, half)
        else:
            src, dst, off = 0, 2 if to_y else 1, ((half, 0) if to_y else (0, half))[i]
        return remote(
            grads.at[k, place(src, off, half)], grads.at[k, place(dst, off, half)],
            gat_s.at[k, int(to_y), i], gat_r.at[k, int(to_y), i], (dev, v),
        )

    def gat_wait(k, to_y, i):
        gat_copy(k, to_y, i).wait_recv()

    def grads_start(k):
        for i in range(1, 8):
            stat_copy(k, i).wait_recv()
        tops = stats[k, :, 0, :]
        totals = stats[k, :, 1, :]
        top = jnp.max(tops, axis=0, keepdims=True)
        total = jnp.sum(totals * jnp.exp(tops - top), axis=0, keepdims=True)
        norm = jnp.broadcast_to(top + jnp.log(total), (128, 128)).T[0:rows, 0:1]
        logits = part[k, place(0)]
        weight = weights[k * rows:(k + 1) * rows, :]
        target = target_col[k * rows:(k + 1) * rows, :]
        columns = v * vocab_rows + lax.broadcasted_iota(jnp.int32, (rows, vocab_rows), 1)
        onehot = (target == columns.astype(f32)).astype(f32)
        grads[k, place(0)] = (weight * (jnp.exp(logits - norm) - onehot)).astype(bf16)
        for i in (0, 1):
            for to_y in (False, True):
                gat_copy(k, to_y, i).start()

    def grads_forward(k):
        gat_wait(k, False, 0)
        gat_copy(k, True, 2).start()
        gat_wait(k, True, 0)
        gat_copy(k, False, 2).start()

    def qpair_copy(k, r, n):
        at = pl.ds(r * rows, n * rows)
        return remote(q_pair.at[k, at], q_pair_in.at[k, at], qpair_s.at[k, r], qpair_r.at[k, r], (g, sib))

    def qplane_copy(k, r):
        return remote(
            q_plane.at[k, place(r)], q_plane_in.at[k, place(r)], qplane_s.at[k, r], qplane_r.at[k, r], (peers[r], v)
        )

    def qline_copy(k, r):
        s = peers[r]
        return remote(
            q_plane_in.at[k, place(r)], q_line.at[k, z], qline_s.at[k, r], qline_r.at[k, z], (g, s * 2 + c)
        )

    def terms_start(k, r, n=1):
        at = pl.ds(r * rows, n * rows)
        grad = grads[k, at]
        q_pair[k, at] = jnp.dot(
            grad, head[:, pl.ds(other_col, width)], preferred_element_type=f32
        ).astype(bf16)
        qpair_copy(k, r, n).start()
        q_keep[k, at] = jnp.dot(grad, head[:, pl.ds(col, width)], preferred_element_type=f32)

    def line_start(k, r):
        @pl.when(peers[r] == z)
        def _():
            q_line[k, z] = q_plane_in[k, place(r)]

        @pl.when(peers[r] != z)
        def _():
            qline_copy(k, r).start()

    def terms_send(k, r, n=1):
        qpair_copy(k, r, n).wait_recv()
        for i in range(r, r + n):
            at = place(i)
            total = (q_keep[k, at] + q_pair_in[k, at].astype(f32)).astype(bf16)
            if i == 0:
                q_plane_in[k, at] = total
                line_start(k, 0)
            else:
                q_plane[k, at] = total
                qplane_copy(k, i).start()

    def terms_line(k):
        for r in (1, 2, 3):
            qplane_copy(k, r).wait_recv()
            line_start(k, r)

    def terms_finish(k):
        for s in range(4):
            @pl.when(s != z)
            def _():
                remote(q_line.at[k, s], q_line.at[k, s], qline_s.at[k, s], qline_r.at[k, s], (g, v)).wait_recv()
        total = q_line[k, 0].astype(f32)
        for s in range(1, 4):
            total = total + q_line[k, s].astype(f32)
        out_hidden[k * rows:(k + 1) * rows, :] = total.astype(bf16)

    def token_columns():
        n = target_ref.shape[1]
        eye = lax.broadcasted_iota(jnp.int32, (n, n), 0) == lax.broadcasted_iota(jnp.int32, (n, n), 1)
        segment = segment_ref[...].astype(f32)
        mask = mask_ref[...].astype(f32)

        def column(row):
            return jnp.sum(jnp.where(eye, row, 0.0), axis=1, keepdims=True)

        counts = jnp.sum(jnp.where(column(segment) == segment, mask, 0.0), axis=1, keepdims=True)
        weights[...] = loss_scale * column(mask) / jnp.maximum(counts, 1.0)
        target_col[...] = column(target_ref[...].astype(f32))

    def stage_a(k):
        hidden_plane(k)
        if k == 0:
            head_copy.wait()
        logits_start(k)

    def stage_d(k):
        grads_start(k)
        terms_start(k, 0)

    def stage_e(k):
        grads_forward(k)
        terms_send(k, 0)
        gat_wait(k, False, 1)
        gat_wait(k, True, 1)
        terms_start(k, 1, 2)

    def stage_f(k):
        gat_wait(k, False, 2)
        gat_wait(k, True, 2)
        terms_start(k, 3)
        terms_send(k, 1, 2)

    def stage_g(k):
        terms_send(k, 3)

    hidden_first(0)
    hidden_first(1)
    token_columns()
    hidden_line(0)
    hidden_first(2)
    hidden_line(1)
    stage_a(0)
    hidden_line(2)
    stage_a(1)
    logits_forward(0)
    stage_a(2)
    logits_forward(1)
    logits_finish(0)
    logits_forward(2)
    stage_d(0)
    logits_finish(1)
    stage_e(0)
    stage_d(1)
    logits_finish(2)
    stage_f(0)
    stage_e(1)
    stage_d(2)
    stage_g(0)
    terms_line(0)
    stage_f(1)
    stage_e(2)
    stage_g(1)
    terms_line(1)
    stage_f(2)
    stage_g(2)
    terms_line(2)

    tiles = 5
    tile_cols = ghead.shape[1] // tiles
    for n in range(tiles):
        at = pl.ds(n * tile_cols, tile_cols)
        total = None
        for k in range(CHUNKS):
            term = lax.dot_general(
                grads[k], mine[k, :, at], (((0,), (0,)), ((), ())), preferred_element_type=f32
            )
            total = term if total is None else total + term
        ghead[:, at] = total.astype(bf16)
    out_copy = pltpu.make_async_copy(ghead, out_head, out_sem)
    out_copy.start()

    for k in range(CHUNKS):
        terms_finish(k)
    for k in range(CHUNKS):
        hidden_finish(k)
        for way in (0, 1):
            for i in (0, 1, 2):
                red_copy(k, way, i).wait_send()
                gat_copy(k, way, i).wait_send()
        for i in range(1, 8):
            stat_copy(k, i).wait_send()
        for r, n in ((0, 1), (1, 2), (3, 1)):
            qpair_copy(k, r, n).wait_send()
        for r in (1, 2, 3):
            qplane_copy(k, r).wait_send()
        for r in range(4):
            @pl.when(peers[r] != z)
            def _():
                qline_copy(k, r).wait_send()
    out_copy.wait()


def fused(hidden, head, targets, segments, loss_mask):
    tokens, width = hidden.shape
    vocab_rows, head_width = head.shape
    rows = tokens // CHUNKS
    half = rows // 2
    bf16, f32 = jnp.bfloat16, jnp.float32
    dma = pltpu.SemaphoreType.DMA
    vmem = pl.BlockSpec(memory_space=pltpu.VMEM)
    hbm = pl.BlockSpec(memory_space=pltpu.HBM)
    anywhere = pl.BlockSpec(memory_space=pl.ANY)
    K = CHUNKS
    return pl.pallas_call(
        functools.partial(kernel, rows, width, vocab_rows),
        out_shape=(
            jax.ShapeDtypeStruct(hidden.shape, bf16),
            jax.ShapeDtypeStruct(head.shape, bf16),
        ),
        in_specs=[hbm, hbm, vmem, vmem, vmem],
        out_specs=(vmem, anywhere),
        scratch_shapes=[
            pltpu.VMEM(head.shape, bf16),
            pltpu.VMEM((K, 4, rows, width), bf16),
            pltpu.VMEM((K, 4 * rows, head_width), bf16),
            pltpu.VMEM((K, 4 * rows, vocab_rows), f32),
            pltpu.VMEM((K, 3, half, vocab_rows), f32),
            pltpu.VMEM((K, 3, half, vocab_rows), f32),
            pltpu.VMEM((128, 128), f32),
            pltpu.VMEM((K, 8, 8, 128), f32),
            pltpu.VMEM((K, 4 * rows, vocab_rows), bf16),
            pltpu.VMEM((tokens, 1), f32),
            pltpu.VMEM((tokens, 1), f32),
            pltpu.VMEM((K, 4 * rows, width), f32),
            pltpu.VMEM((K, 4 * rows, width), bf16),
            pltpu.VMEM((K, 4 * rows, width), bf16),
            pltpu.VMEM((K, 4 * rows, width), bf16),
            pltpu.VMEM((K, 4 * rows, width), bf16),
            pltpu.VMEM((K, 4, rows, width), bf16),
            pltpu.VMEM(head.shape, bf16),
            dma, dma, dma((K,)), dma((K,)),
            dma((K, 2, 3)), dma((K, 2, 3)),
            dma((K, 4)), dma((K, 4)), dma((K, 4)), dma((K, 4)),
            dma((K, 2, 3)), dma((K, 2, 3)),
            dma((K, 7)), dma((K, 7)),
            dma((K, 2, 3)), dma((K, 2, 3)),
            dma((K, 4)), dma((K, 4)), dma((K, 4)), dma((K, 4)), dma((K, 4)), dma((K, 4)),
        ],
        compiler_params=pltpu.CompilerParams(
            collective_id=0, has_side_effects=True, vmem_limit_bytes=40 * 1024 * 1024
        ),
        cost_estimate=pl.CostEstimate(
            flops=3 * 2 * 4 * tokens * vocab_rows * head_width,
            bytes_accessed=4 * vocab_rows * head_width,
            transcendentals=2 * tokens * vocab_rows,
        ),
    )(hidden, head, targets, segments, loss_mask)


def body(hidden, head, targets, segments, loss_mask):
    vocab_rows = head.shape[0]
    features = lax.all_gather(hidden, "vocab", axis=1, tiled=True)
    wide_head = lax.all_gather(head, "dp", axis=1, tiled=True)
    logits = lax.dot_general(
        features, wide_head, (((1,), (1,)), ((), ())), preferred_element_type=jnp.float32
    )
    local_max = jnp.max(logits, axis=1)
    row_max = lax.pmax(local_max, "vocab")
    row_total = lax.psum(jnp.sum(jnp.exp(logits - row_max[:, None]), axis=1), "vocab")
    log_norm = row_max + jnp.log(row_total)
    weight = token_weight(segments, loss_mask)
    vocab_start = lax.axis_index("vocab") * vocab_rows
    columns = vocab_start + lax.broadcasted_iota(jnp.int32, (1, vocab_rows), 1)
    onehot = (targets[0][:, None] == columns).astype(jnp.float32)
    grad_logits = (weight[:, None] * (jnp.exp(logits - log_norm[:, None]) - onehot)).astype(
        jnp.bfloat16
    )
    partial_terms = jnp.dot(grad_logits, wide_head, preferred_element_type=jnp.float32)
    grad_hidden = lax.psum_scatter(partial_terms, "vocab", scatter_dimension=1, tiled=True).astype(
        jnp.bfloat16
    )
    group_cols = lax.all_to_all(features, "dp", split_axis=1, concat_axis=0, tiled=True)
    head_total = lax.dot_general(
        lax.all_gather(grad_logits, "dp", axis=0, tiled=True),
        group_cols,
        (((0,), (0,)), ((), ())),
        preferred_element_type=jnp.float32,
    )
    return (grad_hidden, head_total.astype(jnp.bfloat16))


def solution(mesh):
    placed = (P("dp", "vocab"), P("vocab", "dp"), P("dp", None), P("dp", None), P("dp", None))
    fits = mesh.shape["dp"] == 4 and mesh.shape["vocab"] == 8
    return jax.shard_map(
        fused if fits else body,
        mesh=mesh,
        in_specs=placed,
        out_specs=(P("dp", "vocab"), P("vocab", "dp")),
        check_vma=False,
    )
```

time: 110 us -> 96.5 us (0.88)
  Pallas kernels: 99.9 us -> 88.9 us
  other arithmetic: 2.31 us -> 0 us
    pallas_call x1, Pallas kernels: 99.9 us -> 88.9 us  [fused(): pl.pallas_call(functools.partial(kernel, rows, width, vocab_rows), out_sh...]
    unnamed x2 -> x12, local copies, waits for them, and re-layouts: 4.84 us -> 6.7 us
    another operation x1 -> x0, local copies, waits for them, and re-layouts: 1.44 us -> none  [fused(): target = targets[0][:, None]]
where the time goes in v2:
time: 96.5 us; the launch traced here: 96.2 us
  Pallas kernels  88.9 us (92%)
  local copies, waits for them, and re-layouts  6.7 us (7%)
    pallas_call x1, Pallas kernels, fused(): pl.pallas_call(functools.partial(kernel, rows, width, vocab_rows), out_sh...  88.9 us
    unnamed x12, local copies, waits for them, and re-layouts  6.7 us

profile of v2, /device:TPU:6, one launch (start us, length us, event | category | flops | bytes accessed | tf_op | source)
XLA Modules:
  0.0 96.2 jit_solution(1072874735404220894)
XLA Ops:
  0.6 0.0 copy-start
  0.6 1.6 %copy-done = bf16[896,1280]{1,0:T(8,128)(2,1)S(1)} copy-done((bf16[896,1280]{1,0:T(8,128)(2,1)S(1)}, bf16[896,1280]{1,0:T(8,128)(2,1)}, u32[]{:S(2)}) %copy-start) | copy-done | bytes 2293784
  2.3 0.0 copy-start.1
  2.3 0.9 copy-done.1
  3.2 0.0 copy-start.2
  3.2 0.7 copy-done.2
  3.9 0.0 copy-start.3
  3.9 0.7 copy-done.3
  4.6 0.0 copy-start.4
  4.6 0.7 copy-done.4
  5.3 88.9 %shard_map.68 = (bf16[192,640]{1,0:T(8,128)(2,1)S(1)}, bf16[896,1280]{1,0:T(8,128)(2,1)S(1)}) custom-call(bf16[192,640]{1,0:T(8,128)(2,1)S(1)} %copy-done.1, bf16[896,1280]{1,0:T(8,128)(2,1)S(1)} %copy-done, s32[1,192]{1,0:T(1,128)S(1)} %copy-done.2, s32[1,192]{1,0:T(1,128)S(1)} %copy-done.3, s32[1,192]{1,0:T(1,128)S(1)} %copy-done.4), custom_call_target="tpu_custom_call" | custom-call | flops 5284823040 | bytes 4587520 | tf_op jit(solution)/shard_map/pallas_call | solution.py:430
  94.2 0.7 copy.9
  94.8 1.4 %copy.10 = bf16[896,1280]{1,0:T(8,128)(2,1)} copy(bf16[896,1280]{1,0:T(8,128)(2,1)S(1)} %get-tuple-element.5) | data formatting | bytes 4587520
Async XLA Ops:
  0.6 1.6 %copy-start = (bf16[896,1280]{1,0:T(8,128)(2,1)S(1)}, bf16[896,1280]{1,0:T(8,128)(2,1)}, u32[]{:S(2)}) copy-start(bf16[896,1280]{1,0:T(8,128)(2,1)} %head_hbm.1) | copy-start | bytes 6881284
  2.3 0.9 copy-start.1
  3.2 0.7 copy-start.2
  3.9 0.7 copy-start.3
  4.6 0.7 copy-start.4

commit v3 on v2

--- a/solution.py
+++ b/solution.py
@@ -9,7 +9,7 @@
 
 loss_scale = 256.0
 MESH = pl.DeviceIdType.MESH
-CHUNKS = 3
+CHUNKS = (1, 2, 2, 1)
 
 
 def token_weight(segments, loss_mask):
@@ -21,12 +21,12 @@
 
 
 def kernel(
-    rows, width, vocab_rows,
-    hidden_hbm, head_hbm, target_ref, segment_ref, mask_ref,
+    sizes, width, vocab_rows,
+    hidden_hbm, head_hbm, target_hbm, segment_hbm, mask_hbm,
     out_hidden, out_head,
     head, feats, mine, part, recv_a, recv_b, tile, stats, grads, weights, target_col,
-    q_keep, q_pair, q_pair_in, q_plane, q_plane_in, q_line, ghead,
-    head_sem, out_sem, hidden_sem, own_sem,
+    q_keep, q_pair, q_pair_in, q_plane, q_plane_in, q_line, early, tokens_ref,
+    head_sem, token_sem, hidden_sem, own_sem,
     line_s, line_r, plane_s, plane_r, pair_s, pair_r,
     red_s, red_r, stat_s, stat_r, gat_s, gat_r,
     qpair_s, qpair_r, qplane_s, qplane_r, qline_s, qline_r,
@@ -38,7 +38,8 @@
     xn, yn, dn = gy * 2 + 1 - gx, (1 - gy) * 2 + gx, (1 - gy) * 2 + 1 - gx
     peers = (g, xn, yn, dn)
     sib = z * 2 + 1 - c
-    half = rows // 2
+    chunks = len(sizes)
+    starts = [sum(sizes[:k]) for k in range(chunks)]
     col = pl.multiple_of(c * width, 128)
     other_col = pl.multiple_of((1 - c) * width, 128)
     f32, bf16 = jnp.float32, jnp.bfloat16
@@ -49,16 +50,27 @@
             device_id=dev, device_id_type=MESH,
         )
 
-    def place(r, off=0, n=None):
-        return pl.ds(r * rows + off, rows if n is None else n)
+    def place(k, r, part=None, bins=1):
+        if part is None:
+            return pl.ds(r * sizes[k], bins * sizes[k])
+        return pl.ds(r * sizes[k] + part * (sizes[k] // 2), sizes[k] // 2)
+
+    def own_rows(k):
+        return pl.ds(starts[k], sizes[k])
 
     def hidden_copy(k):
         return pltpu.make_async_copy(
-            hidden_hbm.at[pl.ds(k * rows, rows)], feats.at[k, z], hidden_sem.at[k]
-        )
-
-    for k in range(CHUNKS):
+            hidden_hbm.at[own_rows(k)], feats.at[k, z, pl.ds(0, sizes[k])], hidden_sem.at[k]
+        )
+
+    for k in range(chunks):
         hidden_copy(k).start()
+    token_copies = [
+        pltpu.make_async_copy(ref, tokens_ref.at[i], token_sem.at[i])
+        for i, ref in enumerate((target_hbm, segment_hbm, mask_hbm))
+    ]
+    for copy in token_copies:
+        copy.start()
     head_copy = pltpu.make_async_copy(head_hbm, head, head_sem)
     head_copy.start()
 
@@ -68,7 +80,7 @@
     for i in range(1, 8):
         pl.semaphore_signal(barrier, inc=1, device_id=(g, lax.rem(v + i, 8)), device_id_type=MESH)
     tile[...] = jnp.ones_like(tile)
-    for k in range(CHUNKS):
+    for k in range(chunks):
         hidden_copy(k).wait()
     pl.semaphore_wait(barrier, 10)
 
@@ -76,7 +88,7 @@
         step = 1 if right else -1
         s = z - step * d
         return remote(
-            feats.at[k, s], feats.at[k, s], line_s.at[k, int(right), d], line_r.at[k, int(right), d],
+            feats.at[k, s, pl.ds(0, sizes[k])], feats.at[k, s, pl.ds(0, sizes[k])], line_s.at[k, int(right), d], line_r.at[k, int(right), d],
             (g, (z + step) * 2 + c),
         )
 
@@ -97,13 +109,15 @@
 
     def plane_copy(k, s):
         r = (gx + s) % 2 + 2 * ((gy + s // 2) % 2)
-        at = pl.ds(pl.multiple_of(r * rows, 16), rows)
+        at = pl.ds(pl.multiple_of(r * sizes[k], 16), sizes[k])
         return remote(
-            feats.at[k, s], mine.at[k, at, pl.ds(col, width)], plane_s.at[k, s], plane_r.at[k, r], (s, v)
+            feats.at[k, s, pl.ds(0, sizes[k])], mine.at[k, at, pl.ds(col, width)], plane_s.at[k, s], plane_r.at[k, r], (s, v)
         )
 
     def own_copy(k):
-        return pltpu.make_async_copy(feats.at[k, g], mine.at[k, place(0), pl.ds(col, width)], own_sem.at[k])
+        return pltpu.make_async_copy(
+            feats.at[k, g, pl.ds(0, sizes[k])], mine.at[k, place(k, 0), pl.ds(col, width)], own_sem.at[k]
+        )
 
     def plane_send(k, s):
         @pl.when(s == g)
@@ -122,7 +136,7 @@
         @pl.when(here)
         def _():
             remote(
-                feats.at[k, s], feats.at[k, s], line_s.at[k, int(right), d - 1],
+                feats.at[k, s, pl.ds(0, sizes[k])], feats.at[k, s, pl.ds(0, sizes[k])], line_s.at[k, int(right), d - 1],
                 line_r.at[k, int(right), d - 1], (g, v),
             ).wait_recv()
             if d < 3:
@@ -130,7 +144,7 @@
             plane_send(k, s)
 
     def pair_copy(k, r):
-        at = mine.at[k, place(r), pl.ds(col, width)]
+        at = mine.at[k, place(k, r), pl.ds(col, width)]
         return remote(at, at, pair_s.at[k, r], pair_r.at[k, r], (g, sib))
 
     def hidden_first(k):
@@ -147,11 +161,11 @@
         own_copy(k).wait()
         pair_copy(k, 0).start()
         for r in (1, 2, 3):
-            at = mine.at[k, place(r), pl.ds(col, width)]
+            at = mine.at[k, place(k, r), pl.ds(col, width)]
             remote(at, at, plane_s.at[k, r], plane_r.at[k, r], (peers[r], v)).wait_recv()
             pair_copy(k, r).start()
         for r in range(4):
-            at = mine.at[k, place(r), pl.ds(other_col, width)]
+            at = mine.at[k, place(k, r), pl.ds(other_col, width)]
             remote(at, at, pair_s.at[k, r], pair_r.at[k, r], (g, sib)).wait_recv()
 
     def hidden_finish(k):
@@ -171,13 +185,13 @@
         r = (3, first, second)[i]
         dev = peers[(first, first, second)[i]]
         return remote(
-            part.at[k, place(r, way * half, half)], buf.at[k, i],
+            part.at[k, place(k, r, way)], buf.at[k, i, pl.ds(0, sizes[k] // 2)],
             red_s.at[k, way, i], red_r.at[k, way, i], (dev, v),
         )
 
     def logits_start(k):
-        part[k] = lax.dot_general(
-            mine[k], head[...], (((1,), (1,)), ((), ())), preferred_element_type=f32
+        part[k, place(k, 0, bins=4)] = lax.dot_general(
+            mine[k, place(k, 0, bins=4)], head[...], (((1,), (1,)), ((), ())), preferred_element_type=f32
         )
         for i in (0, 1):
             for way in (0, 1):
@@ -187,8 +201,8 @@
         for way in (0, 1):
             buf = (recv_a, recv_b)[way]
             red_copy(k, way, 0).wait_recv()
-            at = place((2, 1)[way], way * half, half)
-            part[k, at] = part[k, at] + buf[k, 0]
+            at = place(k, (2, 1)[way], way)
+            part[k, at] = part[k, at] + buf[k, 0, 0:sizes[k] // 2]
             red_copy(k, way, 2).start()
 
     def stat_copy(k, i):
@@ -201,13 +215,13 @@
                 red_copy(k, way, i).wait_recv()
         for way in (0, 1):
             buf = (recv_a, recv_b)[way]
-            at = place(0, way * half, half)
-            part[k, at] = part[k, at] + buf[k, 1] + buf[k, 2]
-        logits = part[k, place(0)]
+            at = place(k, 0, way)
+            part[k, at] = part[k, at] + buf[k, 1, 0:sizes[k] // 2] + buf[k, 2, 0:sizes[k] // 2]
+        logits = part[k, place(k, 0)]
         top = jnp.max(logits, axis=1, keepdims=True)
         total = jnp.sum(jnp.exp(logits - top), axis=1, keepdims=True)
-        lane = lax.broadcasted_iota(jnp.int32, (rows, 128), 1)
-        tile[0:rows, :] = jnp.where(lane == 0, top, total)
+        lane = lax.broadcasted_iota(jnp.int32, (sizes[k], 128), 1)
+        tile[0:sizes[k], :] = jnp.where(lane == 0, top, total)
         stats[k, v] = tile[...].T[0:8, :]
         for i in range(1, 8):
             stat_copy(k, i).start()
@@ -215,11 +229,11 @@
     def gat_copy(k, to_y, i):
         dev = yn if to_y else xn
         if i == 2:
-            src, dst, off = (1, 3, 0) if to_y else (2, 3, half)
+            src, dst, part_i = (1, 3, 0) if to_y else (2, 3, 1)
         else:
-            src, dst, off = 0, 2 if to_y else 1, ((half, 0) if to_y else (0, half))[i]
+            src, dst, part_i = 0, 2 if to_y else 1, ((1, 0) if to_y else (0, 1))[i]
         return remote(
-            grads.at[k, place(src, off, half)], grads.at[k, place(dst, off, half)],
+            grads.at[k, place(k, src, part_i)], grads.at[k, place(k, dst, part_i)],
             gat_s.at[k, int(to_y), i], gat_r.at[k, int(to_y), i], (dev, v),
         )
 
@@ -233,13 +247,13 @@
         totals = stats[k, :, 1, :]
         top = jnp.max(tops, axis=0, keepdims=True)
         total = jnp.sum(totals * jnp.exp(tops - top), axis=0, keepdims=True)
-        norm = jnp.broadcast_to(top + jnp.log(total), (128, 128)).T[0:rows, 0:1]
-        logits = part[k, place(0)]
-        weight = weights[k * rows:(k + 1) * rows, :]
-        target = target_col[k * rows:(k + 1) * rows, :]
-        columns = v * vocab_rows + lax.broadcasted_iota(jnp.int32, (rows, vocab_rows), 1)
+        norm = jnp.broadcast_to(top + jnp.log(total), (128, 128)).T[0:sizes[k], 0:1]
+        logits = part[k, place(k, 0)]
+        weight = weights[own_rows(k), :]
+        target = target_col[own_rows(k), :]
+        columns = v * vocab_rows + lax.broadcasted_iota(jnp.int32, (sizes[k], vocab_rows), 1)
         onehot = (target == columns.astype(f32)).astype(f32)
-        grads[k, place(0)] = (weight * (jnp.exp(logits - norm) - onehot)).astype(bf16)
+        grads[k, place(k, 0)] = (weight * (jnp.exp(logits - norm) - onehot)).astype(bf16)
         for i in (0, 1):
             for to_y in (False, True):
                 gat_copy(k, to_y, i).start()
@@ -251,22 +265,22 @@
         gat_copy(k, False, 2).start()
 
     def qpair_copy(k, r, n):
-        at = pl.ds(r * rows, n * rows)
+        at = place(k, r, bins=n)
         return remote(q_pair.at[k, at], q_pair_in.at[k, at], qpair_s.at[k, r], qpair_r.at[k, r], (g, sib))
 
     def qplane_copy(k, r):
         return remote(
-            q_plane.at[k, place(r)], q_plane_in.at[k, place(r)], qplane_s.at[k, r], qplane_r.at[k, r], (peers[r], v)
+            q_plane.at[k, place(k, r)], q_plane_in.at[k, place(k, r)], qplane_s.at[k, r], qplane_r.at[k, r], (peers[r], v)
         )
 
     def qline_copy(k, r):
         s = peers[r]
         return remote(
-            q_plane_in.at[k, place(r)], q_line.at[k, z], qline_s.at[k, r], qline_r.at[k, z], (g, s * 2 + c)
+            q_plane_in.at[k, place(k, r)], q_line.at[k, z, pl.ds(0, sizes[k])], qline_s.at[k, r], qline_r.at[k, z], (g, s * 2 + c)
         )
 
     def terms_start(k, r, n=1):
-        at = pl.ds(r * rows, n * rows)
+        at = place(k, r, bins=n)
         grad = grads[k, at]
         q_pair[k, at] = jnp.dot(
             grad, head[:, pl.ds(other_col, width)], preferred_element_type=f32
@@ -277,7 +291,7 @@
     def line_start(k, r):
         @pl.when(peers[r] == z)
         def _():
-            q_line[k, z] = q_plane_in[k, place(r)]
+            q_line[k, z, 0:sizes[k]] = q_plane_in[k, place(k, r)]
 
         @pl.when(peers[r] != z)
         def _():
@@ -286,7 +300,7 @@
     def terms_send(k, r, n=1):
         qpair_copy(k, r, n).wait_recv()
         for i in range(r, r + n):
-            at = place(i)
+            at = place(k, i)
             total = (q_keep[k, at] + q_pair_in[k, at].astype(f32)).astype(bf16)
             if i == 0:
                 q_plane_in[k, at] = total
@@ -304,24 +318,27 @@
         for s in range(4):
             @pl.when(s != z)
             def _():
-                remote(q_line.at[k, s], q_line.at[k, s], qline_s.at[k, s], qline_r.at[k, s], (g, v)).wait_recv()
-        total = q_line[k, 0].astype(f32)
+                at = q_line.at[k, s, pl.ds(0, sizes[k])]
+                remote(at, at, qline_s.at[k, s], qline_r.at[k, s], (g, v)).wait_recv()
+        total = q_line[k, 0, 0:sizes[k]].astype(f32)
         for s in range(1, 4):
-            total = total + q_line[k, s].astype(f32)
-        out_hidden[k * rows:(k + 1) * rows, :] = total.astype(bf16)
+            total = total + q_line[k, s, 0:sizes[k]].astype(f32)
+        out_hidden[own_rows(k), :] = total.astype(bf16)
 
     def token_columns():
-        n = target_ref.shape[1]
+        for copy in token_copies:
+            copy.wait()
+        n = tokens_ref.shape[2]
         eye = lax.broadcasted_iota(jnp.int32, (n, n), 0) == lax.broadcasted_iota(jnp.int32, (n, n), 1)
-        segment = segment_ref[...].astype(f32)
-        mask = mask_ref[...].astype(f32)
+        segment = tokens_ref[1].astype(f32)
+        mask = tokens_ref[2].astype(f32)
 
         def column(row):
             return jnp.sum(jnp.where(eye, row, 0.0), axis=1, keepdims=True)
 
         counts = jnp.sum(jnp.where(column(segment) == segment, mask, 0.0), axis=1, keepdims=True)
         weights[...] = loss_scale * column(mask) / jnp.maximum(counts, 1.0)
-        target_col[...] = column(target_ref[...].astype(f32))
+        target_col[...] = column(tokens_ref[0].astype(f32))
 
     def stage_a(k):
         hidden_plane(k)
@@ -349,55 +366,52 @@
     def stage_g(k):
         terms_send(k, 3)
 
+    def head_term(k, at):
+        rows = place(k, 0, bins=4)
+        return lax.dot_general(
+            grads[k, rows], mine[k, rows, at], (((0,), (0,)), ((), ())), preferred_element_type=f32
+        )
+
+    tiles = 5
+    tile_cols = out_head.shape[1] // tiles
+
+    def head_early():
+        for n in range(tiles):
+            at = pl.ds(n * tile_cols, tile_cols)
+            total = head_term(0, at)
+            for k in range(1, chunks - 1):
+                total = total + head_term(k, at)
+            early[:, at] = total
+
+    def head_late():
+        for n in range(tiles):
+            at = pl.ds(n * tile_cols, tile_cols)
+            out_head[:, at] = (early[:, at] + head_term(chunks - 1, at)).astype(bf16)
+
     hidden_first(0)
     hidden_first(1)
     token_columns()
     hidden_line(0)
-    hidden_first(2)
+    for k in range(2, chunks):
+        hidden_first(k)
     hidden_line(1)
-    stage_a(0)
-    hidden_line(2)
-    stage_a(1)
-    logits_forward(0)
-    stage_a(2)
-    logits_forward(1)
-    logits_finish(0)
-    logits_forward(2)
-    stage_d(0)
-    logits_finish(1)
-    stage_e(0)
-    stage_d(1)
-    logits_finish(2)
-    stage_f(0)
-    stage_e(1)
-    stage_d(2)
-    stage_g(0)
-    terms_line(0)
-    stage_f(1)
-    stage_e(2)
-    stage_g(1)
-    terms_line(1)
-    stage_f(2)
-    stage_g(2)
-    terms_line(2)
-
-    tiles = 5
-    tile_cols = ghead.shape[1] // tiles
-    for n in range(tiles):
-        at = pl.ds(n * tile_cols, tile_cols)
-        total = None
-        for k in range(CHUNKS):
-            term = lax.dot_general(
-                grads[k], mine[k, :, at], (((0,), (0,)), ((), ())), preferred_element_type=f32
-            )
-            total = term if total is None else total + term
-        ghead[:, at] = total.astype(bf16)
-    out_copy = pltpu.make_async_copy(ghead, out_head, out_sem)
-    out_copy.start()
-
-    for k in range(CHUNKS):
+    steps = (
+        (1, logits_forward), (0, stage_a), (3, stage_d), (2, logits_finish),
+        (4, stage_e), (5, stage_f), (6, stage_g), (7, terms_line),
+    )
+    for slot in range(chunks + 7):
+        if slot == chunks + 6:
+            head_early()
+        for lag, step in steps:
+            if 0 <= slot - lag < chunks:
+                step(slot - lag)
+        if slot + 2 < chunks:
+            hidden_line(slot + 2)
+    head_late()
+
+    for k in range(chunks):
         terms_finish(k)
-    for k in range(CHUNKS):
+    for k in range(chunks):
         hidden_finish(k)
         for way in (0, 1):
             for i in (0, 1, 2):
@@ -413,28 +427,27 @@
             @pl.when(peers[r] != z)
             def _():
                 qline_copy(k, r).wait_send()
-    out_copy.wait()
 
 
 def fused(hidden, head, targets, segments, loss_mask):
     tokens, width = hidden.shape
     vocab_rows, head_width = head.shape
-    rows = tokens // CHUNKS
+    sizes = [tokens * size // sum(CHUNKS) for size in CHUNKS]
+    rows = max(sizes)
     half = rows // 2
     bf16, f32 = jnp.bfloat16, jnp.float32
     dma = pltpu.SemaphoreType.DMA
     vmem = pl.BlockSpec(memory_space=pltpu.VMEM)
     hbm = pl.BlockSpec(memory_space=pltpu.HBM)
-    anywhere = pl.BlockSpec(memory_space=pl.ANY)
-    K = CHUNKS
+    K = len(CHUNKS)
     return pl.pallas_call(
-        functools.partial(kernel, rows, width, vocab_rows),
+        functools.partial(kernel, sizes, width, vocab_rows),
         out_shape=(
             jax.ShapeDtypeStruct(hidden.shape, bf16),
             jax.ShapeDtypeStruct(head.shape, bf16),
         ),
-        in_specs=[hbm, hbm, vmem, vmem, vmem],
-        out_specs=(vmem, anywhere),
+        in_specs=[hbm] * 5,
+        out_specs=(vmem, vmem),
         scratch_shapes=[
             pltpu.VMEM(head.shape, bf16),
             pltpu.VMEM((K, 4, rows, width), bf16),
@@ -453,8 +466,9 @@
             pltpu.VMEM((K, 4 * rows, width), bf16),
             pltpu.VMEM((K, 4 * rows, width), bf16),
             pltpu.VMEM((K, 4, rows, width), bf16),
-            pltpu.VMEM(head.shape, bf16),
-            dma, dma, dma((K,)), dma((K,)),
+            pltpu.VMEM(head.shape, f32),
+            pltpu.VMEM((3, 1, tokens), jnp.int32),
+            dma, dma((3,)), dma((K,)), dma((K,)),
             dma((K, 2, 3)), dma((K, 2, 3)),
             dma((K, 4)), dma((K, 4)), dma((K, 4)), dma((K, 4)),
             dma((K, 2, 3)), dma((K, 2, 3)),
@@ -470,7 +484,7 @@
             bytes_accessed=4 * vocab_rows * head_width,
             transcendentals=2 * tokens * vocab_rows,
         ),
-    )(hidden, head, targets, segments, loss_mask)
+    )(*[pltpu.with_memory_space_constraint(x, pltpu.HBM) for x in (hidden, head, targets, segments, loss_mask)])
 
 
 def body(hidden, head, targets, segments, loss_mask):

time: 96.5 us -> 94 us (0.974)
  local copies, waits for them, and re-layouts: 6.7 us -> 2.08 us
  Pallas kernels: 88.9 us -> 90.9 us
    unnamed x12 -> x2, local copies, waits for them, and re-layouts: 6.7 us -> 2.08 us
    pallas_call x1, Pallas kernels: 88.9 us -> 90.9 us  [fused(): pl.pallas_call(functools.partial(kernel, sizes, width, vocab_rows), out_s...]
where the time goes in v3:
time: 94 us; the launch traced here: 93.7 us
  Pallas kernels  90.9 us (97%)
  local copies, waits for them, and re-layouts  2.08 us (2%)
    pallas_call x1, Pallas kernels, fused(): pl.pallas_call(functools.partial(kernel, sizes, width, vocab_rows), out_s...  90.9 us
    unnamed x2, local copies, waits for them, and re-layouts  2.08 us

profile of v3, /device:TPU:6, one launch (start us, length us, event | category | flops | bytes accessed | tf_op | source)
XLA Modules:
  0.0 93.7 jit_solution(15949319993221167008)
XLA Ops:
  0.6 90.9 %shard_map.68 = (bf16[192,640]{1,0:T(8,128)(2,1)S(1)}, bf16[896,1280]{1,0:T(8,128)(2,1)S(1)}) custom-call(bf16[192,640]{1,0:T(8,128)(2,1)} %hidden_hbm.1, bf16[896,1280]{1,0:T(8,128)(2,1)} %head_hbm.1, s32[1,192]{1,0:T(1,128)} %target_hbm.1, s32[1,192]{1,0:T(1,128)} %segment_hbm.1, s32[1,192]{1,0:T(1,128)} %mask_hbm.1), custom_call_target="tpu_custom_call" | custom-call | flops 5284823040 | bytes 4587520 | tf_op jit(solution)/shard_map/pallas_call | solution.py:443
  91.6 0.7 copy.9
  92.3 1.4 %copy.10 = bf16[896,1280]{1,0:T(8,128)(2,1)} copy(bf16[896,1280]{1,0:T(8,128)(2,1)S(1)} %get-tuple-element.5) | data formatting | bytes 4587520

commit v4 on v3

--- a/solution.py
+++ b/solution.py
@@ -24,7 +24,7 @@
     sizes, width, vocab_rows,
     hidden_hbm, head_hbm, target_hbm, segment_hbm, mask_hbm,
     out_hidden, out_head,
-    head, feats, mine, part, recv_a, recv_b, tile, stats, grads, weights, target_col,
+    head, head_t, feats, mine, part, recv_a, recv_b, tile, stats, grads, weights, target_col,
     q_keep, q_pair, q_pair_in, q_plane, q_plane_in, q_line, early, tokens_ref,
     head_sem, token_sem, hidden_sem, own_sem,
     line_s, line_r, plane_s, plane_r, pair_s, pair_r,
@@ -52,8 +52,8 @@
 
     def place(k, r, part=None, bins=1):
         if part is None:
-            return pl.ds(r * sizes[k], bins * sizes[k])
-        return pl.ds(r * sizes[k] + part * (sizes[k] // 2), sizes[k] // 2)
+            return pl.ds(4 * starts[k] + r * sizes[k], bins * sizes[k])
+        return pl.ds(4 * starts[k] + r * sizes[k] + part * (sizes[k] // 2), sizes[k] // 2)
 
     def own_rows(k):
         return pl.ds(starts[k], sizes[k])
@@ -109,14 +109,14 @@
 
     def plane_copy(k, s):
         r = (gx + s) % 2 + 2 * ((gy + s // 2) % 2)
-        at = pl.ds(pl.multiple_of(r * sizes[k], 16), sizes[k])
+        at = pl.ds(pl.multiple_of(4 * starts[k] + r * sizes[k], 16), sizes[k])
         return remote(
-            feats.at[k, s, pl.ds(0, sizes[k])], mine.at[k, at, pl.ds(col, width)], plane_s.at[k, s], plane_r.at[k, r], (s, v)
+            feats.at[k, s, pl.ds(0, sizes[k])], mine.at[at, pl.ds(col, width)], plane_s.at[k, s], plane_r.at[k, r], (s, v)
         )
 
     def own_copy(k):
         return pltpu.make_async_copy(
-            feats.at[k, g, pl.ds(0, sizes[k])], mine.at[k, place(k, 0), pl.ds(col, width)], own_sem.at[k]
+            feats.at[k, g, pl.ds(0, sizes[k])], mine.at[place(k, 0), pl.ds(col, width)], own_sem.at[k]
         )
 
     def plane_send(k, s):
@@ -144,7 +144,7 @@
             plane_send(k, s)
 
     def pair_copy(k, r):
-        at = mine.at[k, place(k, r), pl.ds(col, width)]
+        at = mine.at[place(k, r), pl.ds(col, width)]
         return remote(at, at, pair_s.at[k, r], pair_r.at[k, r], (g, sib))
 
     def hidden_first(k):
@@ -161,11 +161,11 @@
         own_copy(k).wait()
         pair_copy(k, 0).start()
         for r in (1, 2, 3):
-            at = mine.at[k, place(k, r), pl.ds(col, width)]
+            at = mine.at[place(k, r), pl.ds(col, width)]
             remote(at, at, plane_s.at[k, r], plane_r.at[k, r], (peers[r], v)).wait_recv()
             pair_copy(k, r).start()
         for r in range(4):
-            at = mine.at[k, place(k, r), pl.ds(other_col, width)]
+            at = mine.at[place(k, r), pl.ds(other_col, width)]
             remote(at, at, pair_s.at[k, r], pair_r.at[k, r], (g, sib)).wait_recv()
 
     def hidden_finish(k):
@@ -185,13 +185,13 @@
         r = (3, first, second)[i]
         dev = peers[(first, first, second)[i]]
         return remote(
-            part.at[k, place(k, r, way)], buf.at[k, i, pl.ds(0, sizes[k] // 2)],
+            part.at[place(k, r, way)], buf.at[k, i, pl.ds(0, sizes[k] // 2)],
             red_s.at[k, way, i], red_r.at[k, way, i], (dev, v),
         )
 
     def logits_start(k):
-        part[k, place(k, 0, bins=4)] = lax.dot_general(
-            mine[k, place(k, 0, bins=4)], head[...], (((1,), (1,)), ((), ())), preferred_element_type=f32
+        part[place(k, 0, bins=4)] = lax.dot_general(
+            mine[place(k, 0, bins=4)], head_t[...], (((1,), (0,)), ((), ())), preferred_element_type=f32
         )
         for i in (0, 1):
             for way in (0, 1):
@@ -202,7 +202,7 @@
             buf = (recv_a, recv_b)[way]
             red_copy(k, way, 0).wait_recv()
             at = place(k, (2, 1)[way], way)
-            part[k, at] = part[k, at] + buf[k, 0, 0:sizes[k] // 2]
+            part[at] = part[at] + buf[k, 0, 0:sizes[k] // 2]
             red_copy(k, way, 2).start()
 
     def stat_copy(k, i):
@@ -216,8 +216,8 @@
         for way in (0, 1):
             buf = (recv_a, recv_b)[way]
             at = place(k, 0, way)
-            part[k, at] = part[k, at] + buf[k, 1, 0:sizes[k] // 2] + buf[k, 2, 0:sizes[k] // 2]
-        logits = part[k, place(k, 0)]
+            part[at] = part[at] + buf[k, 1, 0:sizes[k] // 2] + buf[k, 2, 0:sizes[k] // 2]
+        logits = part[place(k, 0)]
         top = jnp.max(logits, axis=1, keepdims=True)
         total = jnp.sum(jnp.exp(logits - top), axis=1, keepdims=True)
         lane = lax.broadcasted_iota(jnp.int32, (sizes[k], 128), 1)
@@ -233,7 +233,7 @@
         else:
             src, dst, part_i = 0, 2 if to_y else 1, ((1, 0) if to_y else (0, 1))[i]
         return remote(
-            grads.at[k, place(k, src, part_i)], grads.at[k, place(k, dst, part_i)],
+            grads.at[place(k, src, part_i)], grads.at[place(k, dst, part_i)],
             gat_s.at[k, int(to_y), i], gat_r.at[k, int(to_y), i], (dev, v),
         )
 
@@ -248,12 +248,12 @@
         top = jnp.max(tops, axis=0, keepdims=True)
         total = jnp.sum(totals * jnp.exp(tops - top), axis=0, keepdims=True)
         norm = jnp.broadcast_to(top + jnp.log(total), (128, 128)).T[0:sizes[k], 0:1]
-        logits = part[k, place(k, 0)]
+        logits = part[place(k, 0)]
         weight = weights[own_rows(k), :]
         target = target_col[own_rows(k), :]
         columns = v * vocab_rows + lax.broadcasted_iota(jnp.int32, (sizes[k], vocab_rows), 1)
         onehot = (target == columns.astype(f32)).astype(f32)
-        grads[k, place(k, 0)] = (weight * (jnp.exp(logits - norm) - onehot)).astype(bf16)
+        grads[place(k, 0)] = (weight * (jnp.exp(logits - norm) - onehot)).astype(bf16)
         for i in (0, 1):
             for to_y in (False, True):
                 gat_copy(k, to_y, i).start()
@@ -266,32 +266,32 @@
 
     def qpair_copy(k, r, n):
         at = place(k, r, bins=n)
-        return remote(q_pair.at[k, at], q_pair_in.at[k, at], qpair_s.at[k, r], qpair_r.at[k, r], (g, sib))
+        return remote(q_pair.at[at], q_pair_in.at[at], qpair_s.at[k, r], qpair_r.at[k, r], (g, sib))
 
     def qplane_copy(k, r):
         return remote(
-            q_plane.at[k, place(k, r)], q_plane_in.at[k, place(k, r)], qplane_s.at[k, r], qplane_r.at[k, r], (peers[r], v)
+            q_plane.at[place(k, r)], q_plane_in.at[place(k, r)], qplane_s.at[k, r], qplane_r.at[k, r], (peers[r], v)
         )
 
     def qline_copy(k, r):
         s = peers[r]
         return remote(
-            q_plane_in.at[k, place(k, r)], q_line.at[k, z, pl.ds(0, sizes[k])], qline_s.at[k, r], qline_r.at[k, z], (g, s * 2 + c)
+            q_plane_in.at[place(k, r)], q_line.at[k, z, pl.ds(0, sizes[k])], qline_s.at[k, r], qline_r.at[k, z], (g, s * 2 + c)
         )
 
     def terms_start(k, r, n=1):
         at = place(k, r, bins=n)
-        grad = grads[k, at]
-        q_pair[k, at] = jnp.dot(
+        grad = grads[at]
+        q_pair[at] = jnp.dot(
             grad, head[:, pl.ds(other_col, width)], preferred_element_type=f32
         ).astype(bf16)
         qpair_copy(k, r, n).start()
-        q_keep[k, at] = jnp.dot(grad, head[:, pl.ds(col, width)], preferred_element_type=f32)
+        q_keep[at] = jnp.dot(grad, head[:, pl.ds(col, width)], preferred_element_type=f32)
 
     def line_start(k, r):
         @pl.when(peers[r] == z)
         def _():
-            q_line[k, z, 0:sizes[k]] = q_plane_in[k, place(k, r)]
+            q_line[k, z, 0:sizes[k]] = q_plane_in[place(k, r)]
 
         @pl.when(peers[r] != z)
         def _():
@@ -301,12 +301,12 @@
         qpair_copy(k, r, n).wait_recv()
         for i in range(r, r + n):
             at = place(k, i)
-            total = (q_keep[k, at] + q_pair_in[k, at].astype(f32)).astype(bf16)
+            total = (q_keep[at] + q_pair_in[at].astype(f32)).astype(bf16)
             if i == 0:
-                q_plane_in[k, at] = total
+                q_plane_in[at] = total
                 line_start(k, 0)
             else:
-                q_plane[k, at] = total
+                q_plane[at] = total
                 qplane_copy(k, i).start()
 
     def terms_line(k):
@@ -342,62 +342,46 @@
 
     def stage_a(k):
         hidden_plane(k)
-        if k == 0:
-            head_copy.wait()
         logits_start(k)
 
-    def stage_d(k):
-        grads_start(k)
-        terms_start(k, 0)
-
-    def stage_e(k):
-        grads_forward(k)
-        terms_send(k, 0)
-        gat_wait(k, False, 1)
-        gat_wait(k, True, 1)
-        terms_start(k, 1, 2)
-
-    def stage_f(k):
-        gat_wait(k, False, 2)
-        gat_wait(k, True, 2)
-        terms_start(k, 3)
-        terms_send(k, 1, 2)
-
-    def stage_g(k):
-        terms_send(k, 3)
-
-    def head_term(k, at):
-        rows = place(k, 0, bins=4)
+    def stage_terms(k):
+        for i in (1, 2):
+            gat_wait(k, False, i)
+            gat_wait(k, True, i)
+        terms_start(k, 0, 4)
+
+    def stage_send(k):
+        terms_send(k, 0, 4)
+
+    tiles = (pl.ds(0, vocab_rows // 256 * 128), pl.ds(vocab_rows // 256 * 128, vocab_rows - vocab_rows // 256 * 128))
+    last = 4 * starts[-1]
+
+    def head_term(at, rows):
         return lax.dot_general(
-            grads[k, rows], mine[k, rows, at], (((0,), (0,)), ((), ())), preferred_element_type=f32
-        )
-
-    tiles = 5
-    tile_cols = out_head.shape[1] // tiles
+            grads[rows, at], mine[rows, :], (((0,), (0,)), ((), ())), preferred_element_type=f32
+        )
 
     def head_early():
-        for n in range(tiles):
-            at = pl.ds(n * tile_cols, tile_cols)
-            total = head_term(0, at)
-            for k in range(1, chunks - 1):
-                total = total + head_term(k, at)
-            early[:, at] = total
+        for at in tiles:
+            early[at, :] = head_term(at, pl.ds(0, last))
 
     def head_late():
-        for n in range(tiles):
-            at = pl.ds(n * tile_cols, tile_cols)
-            out_head[:, at] = (early[:, at] + head_term(chunks - 1, at)).astype(bf16)
+        for at in tiles:
+            out_head[at, :] = (early[at, :] + head_term(at, pl.ds(last, 4 * sizes[-1]))).astype(bf16)
 
     hidden_first(0)
     hidden_first(1)
     token_columns()
+    head_copy.wait()
+    for n in range(0, vocab_rows, 128):
+        head_t[:, n:n + 128] = head[n:n + 128, :].T
     hidden_line(0)
     for k in range(2, chunks):
         hidden_first(k)
     hidden_line(1)
     steps = (
-        (1, logits_forward), (0, stage_a), (3, stage_d), (2, logits_finish),
-        (4, stage_e), (5, stage_f), (6, stage_g), (7, terms_line),
+        (1, logits_forward), (0, stage_a), (4, grads_forward), (3, grads_start),
+        (6, stage_send), (7, terms_line), (5, stage_terms), (2, logits_finish),
     )
     for slot in range(chunks + 7):
         if slot == chunks + 6:
@@ -419,8 +403,7 @@
                 gat_copy(k, way, i).wait_send()
         for i in range(1, 8):
             stat_copy(k, i).wait_send()
-        for r, n in ((0, 1), (1, 2), (3, 1)):
-            qpair_copy(k, r, n).wait_send()
+        qpair_copy(k, 0, 4).wait_send()
         for r in (1, 2, 3):
             qplane_copy(k, r).wait_send()
         for r in range(4):
@@ -450,21 +433,22 @@
         out_specs=(vmem, vmem),
         scratch_shapes=[
             pltpu.VMEM(head.shape, bf16),
+            pltpu.VMEM(head.shape[::-1], bf16),
             pltpu.VMEM((K, 4, rows, width), bf16),
-            pltpu.VMEM((K, 4 * rows, head_width), bf16),
-            pltpu.VMEM((K, 4 * rows, vocab_rows), f32),
+            pltpu.VMEM((4 * tokens, head_width), bf16),
+            pltpu.VMEM((4 * tokens, vocab_rows), f32),
             pltpu.VMEM((K, 3, half, vocab_rows), f32),
             pltpu.VMEM((K, 3, half, vocab_rows), f32),
             pltpu.VMEM((128, 128), f32),
             pltpu.VMEM((K, 8, 8, 128), f32),
-            pltpu.VMEM((K, 4 * rows, vocab_rows), bf16),
+            pltpu.VMEM((4 * tokens, vocab_rows), bf16),
             pltpu.VMEM((tokens, 1), f32),
             pltpu.VMEM((tokens, 1), f32),
-            pltpu.VMEM((K, 4 * rows, width), f32),
-            pltpu.VMEM((K, 4 * rows, width), bf16),
-            pltpu.VMEM((K, 4 * rows, width), bf16),
-            pltpu.VMEM((K, 4 * rows, width), bf16),
-            pltpu.VMEM((K, 4 * rows, width), bf16),
+            pltpu.VMEM((4 * tokens, width), f32),
+            pltpu.VMEM((4 * tokens, width), bf16),
+            pltpu.VMEM((4 * tokens, width), bf16),
+            pltpu.VMEM((4 * tokens, width), bf16),
+            pltpu.VMEM((4 * tokens, width), bf16),
             pltpu.VMEM((K, 4, rows, width), bf16),
             pltpu.VMEM(head.shape, f32),
             pltpu.VMEM((3, 1, tokens), jnp.int32),

time: 94 us -> 93 us (0.989)
  no operation moved by 1% of the time
where the time goes in v4:
time: 93 us; the launch traced here: 92.9 us
  Pallas kernels  90.2 us (97%)
  local copies, waits for them, and re-layouts  2.08 us (2%)
    pallas_call x1, Pallas kernels, fused(): pl.pallas_call(functools.partial(kernel, sizes, width, vocab_rows), out_s...  90.2 us
    unnamed x2, local copies, waits for them, and re-layouts  2.08 us

profile of v4, /device:TPU:6, one launch (start us, length us, event | category | flops | bytes accessed | tf_op | source)
XLA Modules:
  0.0 92.9 jit_solution(17187178220546588682)
XLA Ops:
  0.6 90.2 %shard_map.68 = (bf16[192,640]{1,0:T(8,128)(2,1)S(1)}, bf16[896,1280]{1,0:T(8,128)(2,1)S(1)}) custom-call(bf16[192,640]{1,0:T(8,128)(2,1)} %hidden_hbm.1, bf16[896,1280]{1,0:T(8,128)(2,1)} %head_hbm.1, s32[1,192]{1,0:T(1,128)} %target_hbm.1, s32[1,192]{1,0:T(1,128)} %segment_hbm.1, s32[1,192]{1,0:T(1,128)} %mask_hbm.1), custom_call_target="tpu_custom_call" | custom-call | flops 5284823040 | bytes 4587520 | tf_op jit(solution)/shard_map/pallas_call | solution.py:426
  90.8 0.7 copy.9
  91.5 1.4 %copy.10 = bf16[896,1280]{1,0:T(8,128)(2,1)} copy(bf16[896,1280]{1,0:T(8,128)(2,1)S(1)} %get-tuple-element.5) | data formatting | bytes 4587520

commit v5 on v4

--- a/solution.py
+++ b/solution.py
@@ -25,11 +25,11 @@
     hidden_hbm, head_hbm, target_hbm, segment_hbm, mask_hbm,
     out_hidden, out_head,
     head, head_t, feats, mine, part, recv_a, recv_b, tile, stats, grads, weights, target_col,
-    q_keep, q_pair, q_pair_in, q_plane, q_plane_in, q_line, early, tokens_ref,
+    q_keep, q_pair, q_pair_in, q_plane, q_plane_in, q_line, q_relay, early, tokens_ref,
     head_sem, token_sem, hidden_sem, own_sem,
     line_s, line_r, plane_s, plane_r, pair_s, pair_r,
     red_s, red_r, stat_s, stat_r, gat_s, gat_r,
-    qpair_s, qpair_r, qplane_s, qplane_r, qline_s, qline_r,
+    qpair_s, qpair_r, qplane_s, qplane_r, qline_s, qline_r, relay_r,
 ):
     g = lax.axis_index("dp")
     v = lax.axis_index("vocab")
@@ -80,6 +80,11 @@
     for i in range(1, 8):
         pl.semaphore_signal(barrier, inc=1, device_id=(g, lax.rem(v + i, 8)), device_id_type=MESH)
     tile[...] = jnp.ones_like(tile)
+    for k in range(chunks - 1):
+        for s in (0, 3):
+            @pl.when(z == 3 - s)
+            def _():
+                q_line[k, s] = jnp.zeros(q_line.shape[2:], bf16)
     for k in range(chunks):
         hidden_copy(k).wait()
     pl.semaphore_wait(barrier, 10)
@@ -237,6 +242,11 @@
             gat_s.at[k, int(to_y), i], gat_r.at[k, int(to_y), i], (dev, v),
         )
 
+    def gat_direct(k, r):
+        return remote(
+            grads.at[place(k, 0)], grads.at[place(k, r)], gat_s.at[k, 0, r - 1], gat_r.at[k, 0, r - 1], (peers[r], v)
+        )
+
     def gat_wait(k, to_y, i):
         gat_copy(k, to_y, i).wait_recv()
 
@@ -254,11 +264,17 @@
         columns = v * vocab_rows + lax.broadcasted_iota(jnp.int32, (sizes[k], vocab_rows), 1)
         onehot = (target == columns.astype(f32)).astype(f32)
         grads[place(k, 0)] = (weight * (jnp.exp(logits - norm) - onehot)).astype(bf16)
+        if k == chunks - 1:
+            for r in (3, 1, 2):
+                gat_direct(k, r).start()
+            return
         for i in (0, 1):
             for to_y in (False, True):
                 gat_copy(k, to_y, i).start()
 
     def grads_forward(k):
+        if k == chunks - 1:
+            return
         gat_wait(k, False, 0)
         gat_copy(k, True, 2).start()
         gat_wait(k, True, 0)
@@ -293,9 +309,45 @@
         def _():
             q_line[k, z, 0:sizes[k]] = q_plane_in[place(k, r)]
 
-        @pl.when(peers[r] != z)
+        if k == chunks - 1:
+            @pl.when(peers[r] != z)
+            def _():
+                qline_copy(k, r).start()
+
+            return
+
+        s = peers[r]
+        far = ((z == 0) & (s == 3)) | ((z == 3) & (s == 0))
+        held = ((z == 1) & (s == 3)) | ((z == 2) & (s == 0))
+
+        @pl.when(far)
+        def _():
+            remote(
+                q_plane_in.at[place(k, r)], q_relay.at[k, 0, pl.ds(0, sizes[k])], qline_s.at[k, r], relay_r.at[k],
+                (g, (1 + z // 3) * 2 + c),
+            ).start()
+
+        @pl.when((s != z) & jnp.logical_not(far | held))
         def _():
             qline_copy(k, r).start()
+
+    def terms_relay(k):
+        if k == chunks - 1:
+            return
+        n = sizes[k]
+
+        @pl.when((z == 1) | (z == 2))
+        def _():
+            s = 6 - 3 * z
+            r = (gx + s) % 2 + 2 * ((gy + s // 2) % 2)
+            at = q_relay.at[k, 0, pl.ds(0, n)]
+            remote(at, at, qline_s.at[k, r], relay_r.at[k], (g, v)).wait_recv()
+            rows = pl.ds(pl.multiple_of(4 * starts[k] + r * n, 16), n)
+            q_relay[k, 1, 0:n] = (q_plane_in[rows].astype(f32) + q_relay[k, 0, 0:n].astype(f32)).astype(bf16)
+            remote(
+                q_relay.at[k, 1, pl.ds(0, n)], q_line.at[k, z, pl.ds(0, n)], qline_s.at[k, r], qline_r.at[k, z],
+                (g, s * 2 + c),
+            ).start()
 
     def terms_send(k, r, n=1):
         qpair_copy(k, r, n).wait_recv()
@@ -316,7 +368,11 @@
 
     def terms_finish(k):
         for s in range(4):
-            @pl.when(s != z)
+            arrives = s != z
+            if k < chunks - 1 and s in (0, 3):
+                arrives = arrives & (z != 3 - s)
+
+            @pl.when(arrives)
             def _():
                 at = q_line.at[k, s, pl.ds(0, sizes[k])]
                 remote(at, at, qline_s.at[k, s], qline_r.at[k, s], (g, v)).wait_recv()
@@ -345,9 +401,13 @@
         logits_start(k)
 
     def stage_terms(k):
-        for i in (1, 2):
-            gat_wait(k, False, i)
-            gat_wait(k, True, i)
+        if k == chunks - 1:
+            for r in (1, 2, 3):
+                gat_direct(k, r).wait_recv()
+        else:
+            for i in (1, 2):
+                gat_wait(k, False, i)
+                gat_wait(k, True, i)
         terms_start(k, 0, 4)
 
     def stage_send(k):
@@ -381,7 +441,7 @@
     hidden_line(1)
     steps = (
         (1, logits_forward), (0, stage_a), (4, grads_forward), (3, grads_start),
-        (6, stage_send), (7, terms_line), (5, stage_terms), (2, logits_finish),
+        (6, stage_send), (7, terms_line), (8, terms_relay), (5, stage_terms), (2, logits_finish),
     )
     for slot in range(chunks + 7):
         if slot == chunks + 6:
@@ -400,7 +460,11 @@
         for way in (0, 1):
             for i in (0, 1, 2):
                 red_copy(k, way, i).wait_send()
-                gat_copy(k, way, i).wait_send()
+                if k < chunks - 1:
+                    gat_copy(k, way, i).wait_send()
+        if k == chunks - 1:
+            for r in (1, 2, 3):
+                gat_direct(k, r).wait_send()
         for i in range(1, 8):
             stat_copy(k, i).wait_send()
         qpair_copy(k, 0, 4).wait_send()
@@ -450,6 +514,7 @@
             pltpu.VMEM((4 * tokens, width), bf16),
             pltpu.VMEM((4 * tokens, width), bf16),
             pltpu.VMEM((K, 4, rows, width), bf16),
+            pltpu.VMEM((K, 2, rows, width), bf16),
             pltpu.VMEM(head.shape, f32),
             pltpu.VMEM((3, 1, tokens), jnp.int32),
             dma, dma((3,)), dma((K,)), dma((K,)),
@@ -458,7 +523,7 @@
             dma((K, 2, 3)), dma((K, 2, 3)),
             dma((K, 7)), dma((K, 7)),
             dma((K, 2, 3)), dma((K, 2, 3)),
-            dma((K, 4)), dma((K, 4)), dma((K, 4)), dma((K, 4)), dma((K, 4)), dma((K, 4)),
+            dma((K, 4)), dma((K, 4)), dma((K, 4)), dma((K, 4)), dma((K, 4)), dma((K, 4)), dma((K,)),
         ],
         compiler_params=pltpu.CompilerParams(
             collective_id=0, has_side_effects=True, vmem_limit_bytes=40 * 1024 * 1024

time: 93 us -> 93.9 us (level)
  no operation moved by 1% of the time
where the time goes in v5:
time: 93.9 us; the launch traced here: 93.2 us
  Pallas kernels  90.5 us (96%)
  local copies, waits for them, and re-layouts  2.08 us (2%)
    pallas_call x1, Pallas kernels, fused(): pl.pallas_call(functools.partial(kernel, sizes, width, vocab_rows), out_s...  90.5 us
    unnamed x2, local copies, waits for them, and re-layouts  2.08 us

profile of v5, /device:TPU:6, one launch (start us, length us, event | category | flops | bytes accessed | tf_op | source)
XLA Modules:
  0.0 93.2 jit_solution(7018136233499557887)
XLA Ops:
  0.6 90.5 %shard_map.68 = (bf16[192,640]{1,0:T(8,128)(2,1)S(1)}, bf16[896,1280]{1,0:T(8,128)(2,1)S(1)}) custom-call(bf16[192,640]{1,0:T(8,128)(2,1)} %hidden_hbm.1, bf16[896,1280]{1,0:T(8,128)(2,1)} %head_hbm.1, s32[1,192]{1,0:T(1,128)} %target_hbm.1, s32[1,192]{1,0:T(1,128)} %segment_hbm.1, s32[1,192]{1,0:T(1,128)} %mask_hbm.1), custom_call_target="tpu_custom_call" | custom-call | flops 5284823040 | bytes 4587520 | tf_op jit(solution)/shard_map/pallas_call | solution.py:490
  91.1 0.7 copy.9
  91.8 1.4 %copy.10 = bf16[896,1280]{1,0:T(8,128)(2,1)} copy(bf16[896,1280]{1,0:T(8,128)(2,1)S(1)} %get-tuple-element.5) | data formatting | bytes 4587520

commit v6 on v4

--- a/solution.py
+++ b/solution.py
@@ -152,10 +152,9 @@
         line_send(k, False, 0)
         plane_send(k, z)
 
-    def hidden_line(k):
-        for d in (1, 2, 3):
-            line_recv(k, True, d)
-            line_recv(k, False, d)
+    def hidden_line(k, d):
+        line_recv(k, True, d)
+        line_recv(k, False, d)
 
     def hidden_plane(k):
         own_copy(k).wait()
@@ -369,16 +368,31 @@
         for at in tiles:
             out_head[at, :] = (early[at, :] + head_term(at, pl.ds(last, 4 * sizes[-1]))).astype(bf16)
 
+    def turn(n):
+        at = pl.ds(n * 128, 128)
+        head_t[:, at] = head[at, :].T
+
     hidden_first(0)
     hidden_first(1)
     token_columns()
     head_copy.wait()
-    for n in range(0, vocab_rows, 128):
-        head_t[:, n:n + 128] = head[n:n + 128, :].T
-    hidden_line(0)
-    for k in range(2, chunks):
-        hidden_first(k)
-    hidden_line(1)
+    pieces = iter(range(vocab_rows // 128))
+    for k in (0, 1):
+        for d in (1, 2, 3):
+            hidden_line(k, d)
+            for n in (next(pieces, None),):
+                if n is not None:
+                    turn(n)
+        if k == 0:
+            for later in range(2, chunks):
+                hidden_first(later)
+    for n in pieces:
+        turn(n)
+    arrivals = {
+        (stage_a, 0): ((2, 2),), (logits_forward, 0): ((3, 1),),
+        (stage_a, 1): ((2, 3), (3, 2)), (stage_a, 2): ((3, 3),),
+    }
+    hidden_line(2, 1)
     steps = (
         (1, logits_forward), (0, stage_a), (4, grads_forward), (3, grads_start),
         (6, stage_send), (7, terms_line), (5, stage_terms), (2, logits_finish),
@@ -389,8 +403,8 @@
         for lag, step in steps:
             if 0 <= slot - lag < chunks:
                 step(slot - lag)
-        if slot + 2 < chunks:
-            hidden_line(slot + 2)
+                for k, d in arrivals.get((step, slot - lag), ()):
+                    hidden_line(k, d)
     head_late()
 
     for k in range(chunks):

time: 93 us -> 96.6 us (1.039)
  Pallas kernels: 90.2 us -> 93.7 us
    pallas_call x1, Pallas kernels: 90.2 us -> 93.7 us  [fused(): pl.pallas_call(functools.partial(kernel, sizes, width, vocab_rows), out_s...]
where the time goes in v6:
time: 96.6 us; the launch traced here: 96.4 us
  Pallas kernels  93.7 us (97%)
  local copies, waits for them, and re-layouts  2.08 us (2%)
    pallas_call x1, Pallas kernels, fused(): pl.pallas_call(functools.partial(kernel, sizes, width, vocab_rows), out_s...  93.7 us
    unnamed x2, local copies, waits for them, and re-layouts  2.08 us

profile of v6, /device:TPU:6, one launch (start us, length us, event | category | flops | bytes accessed | tf_op | source)
XLA Modules:
  0.0 96.4 jit_solution(2036943043824217045)
XLA Ops:
  0.6 93.7 %shard_map.68 = (bf16[192,640]{1,0:T(8,128)(2,1)S(1)}, bf16[896,1280]{1,0:T(8,128)(2,1)S(1)}) custom-call(bf16[192,640]{1,0:T(8,128)(2,1)} %hidden_hbm.1, bf16[896,1280]{1,0:T(8,128)(2,1)} %head_hbm.1, s32[1,192]{1,0:T(1,128)} %target_hbm.1, s32[1,192]{1,0:T(1,128)} %segment_hbm.1, s32[1,192]{1,0:T(1,128)} %mask_hbm.1), custom_call_target="tpu_custom_call" | custom-call | flops 5284823040 | bytes 4587520 | tf_op jit(solution)/shard_map/pallas_call | solution.py:440
  94.3 0.7 copy.9
  95.0 1.4 %copy.10 = bf16[896,1280]{1,0:T(8,128)(2,1)} copy(bf16[896,1280]{1,0:T(8,128)(2,1)S(1)} %get-tuple-element.5) | data formatting | bytes 4587520
